TPU v7x, 32 devices: a whole 2x2x4 slice. The times are simulated.
32 devices in a mesh: sky: 2 (over x), tm: 16 (over z, y, core).
Axes of the slice: x: 2, y: 2, z: 4, core: 2. Of those that a mesh axis runs over, the one named last changes fastest.
Arguments:
- series: bfloat16 [4, 4, 1024, 2048], P('sky', None, 'tm'), parts along dimension 0, may hold values from -6 to 6
- antenna: float32 [4, 3], P('sky'), parts along dimension 0, as said below
- offsets: int32 [16, 2], P('sky'), parts along dimension 0, may hold values from -8 to 8, as said below
Outputs:
- detection: float32 [16, 1024, 2048], P('sky', 'tm'), parts along dimension 0
There are 2 independent parts, one for each index of `sky`. A program takes and returns all parts, laid end to end along the dimension named above; each array names one. Nothing has to cross between parts.
Inputs may be any that keep to these rules, and one draw needn't show every extreme that they name: `offsets`: both -8 and 8 occur in every draw. `antenna`: A and B are positive and C C is at most 0.49 A B in every row.
All inputs are finite; a program needn't handle non-finite values.
Results may differ from a plain program's by a relative error of at most 0.0032.
Values may be sent and summed in bfloat16 or wider, within the bound.
No kernel may reach another device: no remote copies, remote signals or barrier semaphores. Data moves between devices by JAX's collectives and lax.ppermute only.
A program may use at most 128 MiB of HBM per device.

v0:
```python
import math

import jax
import jax.numpy as jnp
from jax import lax
from jax.sharding import PartitionSpec as P

NA = 2048
NB = 1024
LEN = 2097152
DMAX = 8


def with_halo(cells, sides, width):
    for axis, dim in sides:
        count = lax.axis_size(axis)
        head = lax.slice_in_dim(cells, 0, width, axis=dim)
        tail = lax.slice_in_dim(cells, cells.shape[dim] - width, cells.shape[dim], axis=dim)
        cells = jnp.concatenate(
            [
                lax.ppermute(tail, axis, [(i, (i + 1) % count) for i in range(count)]),
                cells,
                lax.ppermute(head, axis, [((i + 1) % count, i) for i in range(count)]),
            ],
            axis=dim,
        )
    return cells


def dft_table(length):
    indices = jnp.arange(length, dtype=jnp.int32)
    products = indices[:, None] * indices[None, :] % length
    phase_angle = products.astype(jnp.float32) * (2.0 * math.pi / length)
    return (jnp.cos(phase_angle).astype(jnp.bfloat16), (-jnp.sin(phase_angle)).astype(jnp.bfloat16))


def complex_dft(x_real, x_imag, w_real, w_imag, formula):
    real_part = jnp.einsum(
        formula, x_real, w_real, preferred_element_type=jnp.float32
    ) - jnp.einsum(formula, x_imag, w_imag, preferred_element_type=jnp.float32)
    imag_part = jnp.einsum(
        formula, x_real, w_imag, preferred_element_type=jnp.float32
    ) + jnp.einsum(formula, x_imag, w_real, preferred_element_type=jnp.float32)
    return (real_part, imag_part)


def projection(spectra, antenna):
    coef_a = antenna[:, 0][:, None, None]
    coef_b = antenna[:, 1][:, None, None]
    coef_c = antenna[:, 2][:, None, None]
    a_real, a_imag, b_real, b_imag = (spectra[:, 0], spectra[:, 1], spectra[:, 2], spectra[:, 3])
    numer = (
        coef_b * (a_real * a_real + a_imag * a_imag)
        + coef_a * (b_real * b_real + b_imag * b_imag)
        - 2.0 * coef_c * (a_real * b_real + a_imag * b_imag)
    )
    return numer / ((coef_a * coef_b - coef_c * coef_c) * LEN)


def carry_rims(widened, my_index, group_size):
    lower_rim = widened[..., :DMAX, :]
    upper_rim = widened[..., widened.shape[-2] - DMAX :, :]
    middle = widened[..., DMAX : widened.shape[-2] - DMAX, :]
    lower_rim = jnp.where(my_index == 0, jnp.roll(lower_rim, 1, axis=-1), lower_rim)
    upper_rim = jnp.where(my_index == group_size - 1, jnp.roll(upper_rim, -1, axis=-1), upper_rim)
    return jnp.concatenate([lower_rim, middle, upper_rim], axis=-2)


def local(series, antenna, offsets):
    group_size = lax.axis_size("tm")
    my_index = lax.axis_index("tm")
    seg_count = series.shape[0]
    col_block = NA // group_size
    row_block = NB // group_size
    short_real, short_imag = dft_table(NB)
    long_real, long_imag = dft_table(NA)
    columns = my_index * col_block + jnp.arange(col_block, dtype=jnp.int32)
    bins = jnp.arange(NB, dtype=jnp.int32)
    twist = (columns[:, None] * bins[None, :] % LEN).astype(jnp.float32) * (2.0 * math.pi / LEN)
    twid_real = jnp.cos(twist)
    twid_imag = -jnp.sin(twist)
    members = lax.all_to_all(series, "tm", split_axis=3, concat_axis=2, tiled=True)
    pieces = []
    for lead in (0, 2):
        real_part, imag_part = complex_dft(
            members[:, lead], members[:, lead + 1], short_real, short_imag, "snj,nk->sjk"
        )
        pieces.append((real_part * twid_real - imag_part * twid_imag).astype(jnp.bfloat16))
        pieces.append((real_part * twid_imag + imag_part * twid_real).astype(jnp.bfloat16))
    twiddled = jnp.stack(pieces, axis=1)
    members = lax.all_to_all(twiddled, "tm", split_axis=3, concat_axis=2, tiled=True)
    pieces = []
    for lead in (0, 2):
        real_part, imag_part = complex_dft(
            members[:, lead], members[:, lead + 1], long_real, long_imag, "sjk,jm->skm"
        )
        pieces.append(real_part)
        pieces.append(imag_part)
    spectra = jnp.stack(pieces, axis=1)
    local_fstat = projection(spectra, antenna)
    widened = with_halo(local_fstat, (("tm", 1),), DMAX)
    fstat = carry_rims(widened, my_index, group_size)

    def one_template(shift_row):
        total_sum = jnp.zeros((row_block, fstat.shape[-1]), jnp.float32)
        for segment in range(seg_count):
            total_sum = total_sum + lax.dynamic_slice_in_dim(
                fstat[segment], DMAX + shift_row[segment], row_block, 0
            )
        return total_sum / seg_count

    return jax.vmap(one_template)(offsets)


def solution(mesh):
    return jax.shard_map(
        local,
        mesh=mesh,
        in_specs=(P("sky", None, "tm", None), P("sky", None), P("sky", None)),
        out_specs=P("sky", "tm", None),
        check_vma=False,
    )
```

profile of v0, /device:TPU:0, one launch (start us, length us, event | category | flops | bytes accessed | tf_op | source)
XLA Modules:
  0.0 823.1 jit_solution(13590699504067278023)
XLA Ops:
  0.0 7.0 copy.6
  7.0 7.5 reshape.137
  14.5 7.4 all-to-all-start
  24.0 39.0 %all-to-all-done = bf16[16,2,32768]{2,1,0:T(2,128)(2,1)S(1)} async-done(((bf16[16,2,32768]{2,1,0:T(2,128)(2,1)}), bf16[16,2,32768]{2,1,0:T(2,128)(2,1)S(1)}, u32[]{:S(2)}, u32[]{:S(2)}) %all-to-all-start) | async-done | bytes 2097184 | tf_op jit(solution)/shard_map/all_to_all | solution.py:82
  63.0 4.9 reshape.138
  67.9 6.0 copy.7
  73.9 16.2 %fusion.44 = f32[1024,2,128]{2,0,1:T(8,128)S(1)} fusion(bf16[2,4,1024,128]{3,2,0,1:T(8,128)(2,1)S(1)} %bitcast.189), kind=kOutput, calls=%fused_computation.45 | convolution fusion | flops 553648128 | bytes 1572864 | tf_op jit(solution)/shard_map/snj,nk->sjk/dot_general | solution.py:41
  90.1 16.0 %fusion.48 = f32[1024,2,128]{2,0,1:T(8,128)S(1)} fusion(bf16[2,4,1024,128]{3,2,0,1:T(8,128)(2,1)S(1)} %bitcast.190), kind=kOutput, calls=%fused_computation.47 | convolution fusion | flops 553648128 | bytes 1572864 | tf_op jit(solution)/shard_map/snj,nk->sjk/dot_general | solution.py:41
  106.2 16.5 %fusion.46 = f32[1024,2,128]{2,0,1:T(8,128)S(1)} fusion(bf16[2,4,1024,128]{3,2,0,1:T(8,128)(2,1)S(1)} %bitcast.191), kind=kOutput, calls=%fused_computation.46 | convolution fusion | flops 553648128 | bytes 1572864 | tf_op jit(solution)/shard_map/snj,nk->sjk/dot_general | solution.py:40
  122.6 16.0 %fusion.50 = f32[1024,2,128]{2,0,1:T(8,128)S(1)} fusion(bf16[2,4,1024,128]{3,2,0,1:T(8,128)(2,1)S(1)} %bitcast.192), kind=kOutput, calls=%fused_computation.48 | convolution fusion | flops 553648128 | bytes 1572864 | tf_op jit(solution)/shard_map/snj,nk->sjk/dot_general | solution.py:40
  138.6 15.8 %fusion.69 = f32[2,128,1024]{1,2,0:T(8,128)S(1)} fusion(f32[1024,2,128]{2,0,1:T(8,128)S(1)} %fusion.48, bf16[2,4,1024,128]{3,2,0,1:T(8,128)(2,1)S(1)} %bitcast.193), kind=kOutput, calls=%fused_computation.56 | convolution fusion | flops 552861696 | bytes 2621440 | tf_op jit(solution)/shard_map/snj,nk->sjk/dot_general | solution.py:43
  154.5 16.2 %fusion.75 = f32[2,128,1024]{1,2,0:T(8,128)S(1)} fusion(f32[1024,2,128]{2,0,1:T(8,128)S(1)} %fusion.46, bf16[2,4,1024,128]{3,2,0,1:T(8,128)(2,1)S(1)} %bitcast.194), kind=kOutput, calls=%fused_computation.58 | convolution fusion | flops 552861696 | bytes 2621440 | tf_op jit(solution)/shard_map/snj,nk->sjk/dot_general | solution.py:38
  170.7 15.8 %fusion.63 = f32[2,128,1024]{1,2,0:T(8,128)S(1)} fusion(f32[1024,2,128]{2,0,1:T(8,128)S(1)} %fusion.50, bf16[2,4,1024,128]{3,2,0,1:T(8,128)(2,1)S(1)} %bitcast.195), kind=kOutput, calls=%fused_computation.54 | convolution fusion | flops 552861696 | bytes 2621440 | tf_op jit(solution)/shard_map/snj,nk->sjk/dot_general | solution.py:38
  186.5 18.2 %fusion.89 = (bf16[2,1,128,1024]{2,3,0,1:T(8,128)(2,1)S(1)}, bf16[2,1,128,1024]{2,3,0,1:T(8,128)(2,1)S(1)}, bf16[2,1,128,1024]{2,3,0,1:T(8,128)(2,1)S(1)}, bf16[2,1,128,1024]{2,3,0,1:T(8,128)(2,1)S(1)}) fusion(f32[2,128,1024]{1,2,0:T(8,128)S(1)} %fusion.69, f32[2,128,1024]{1,2,0:T(8,128)S(1)} %fusion.63, f32[128,1024]{0,1:T(8,128)S(1)} %get-tuple-element.54, ...), kind=kOutput, calls=%fused_computation.75 | convolution fusion | flops 557056000 | bytes 7864320 | tf_op jit(solution)/shard_map/snj,nk->sjk/dot_general | solution.py:43
  205.0 3.5 copy.8
  208.5 11.2 %all-to-all-start.1 = ((bf16[2,4,128,1024]{2,0,1,3:T(2,128)(2,1)}), bf16[2,4,128,1024]{2,0,1,3:T(2,128)(2,1)S(1)}, u32[]{:S(2)}, u32[]{:S(2)}) async-start(bf16[2,4,128,1024]{2,0,1,3:T(2,128)(2,1)} %copy.8), calls=%async_computation.1 | async-start | bytes 4194304 | tf_op jit(solution)/shard_map/all_to_all | solution.py:91
  219.9 40.9 %all-to-all-done.1 = bf16[2,4,128,1024]{2,0,1,3:T(2,128)(2,1)S(1)} async-done(((bf16[2,4,128,1024]{2,0,1,3:T(2,128)(2,1)}), bf16[2,4,128,1024]{2,0,1,3:T(2,128)(2,1)S(1)}, u32[]{:S(2)}, u32[]{:S(2)}) %all-to-all-start.1) | async-done | bytes 2097184 | tf_op jit(solution)/shard_map/all_to_all | solution.py:91
  260.8 2.7 copy.11
  263.5 2.8 all_to_all.33
  266.3 62.7 %fusion.8 = f32[2,64,2048]{2,1,0:T(8,128)S(1)} fusion(bf16[2,4,2048,64]{2,3,0,1:T(8,128)(2,1)S(1)} %all_to_all.33), kind=kOutput, calls=%fused_computation.17 | convolution fusion | flops 1140850688 | bytes 1572864 | tf_op jit(solution)/shard_map/sjk,jm->skm/dot_general | solution.py:41
  329.0 63.0 %fusion.12 = f32[2,64,2048]{2,1,0:T(8,128)S(1)} fusion(bf16[2,4,2048,64]{2,3,0,1:T(8,128)(2,1)S(1)} %all_to_all.33), kind=kOutput, calls=%fused_computation.19 | convolution fusion | flops 1140850688 | bytes 1572864 | tf_op jit(solution)/shard_map/sjk,jm->skm/dot_general | solution.py:41
  392.0 62.7 %fusion.10 = f32[2,64,2048]{2,1,0:T(8,128)S(1)} fusion(bf16[2,4,2048,64]{2,3,0,1:T(8,128)(2,1)S(1)} %all_to_all.33), kind=kOutput, calls=%fused_computation.18 | convolution fusion | flops 1140850688 | bytes 1572864 | tf_op jit(solution)/shard_map/sjk,jm->skm/dot_general | solution.py:40
  454.8 63.1 %fusion.14 = f32[2,64,2048]{2,1,0:T(8,128)S(1)} fusion(bf16[2,4,2048,64]{2,3,0,1:T(8,128)(2,1)S(1)} %all_to_all.33), kind=kOutput, calls=%fused_computation.20 | convolution fusion | flops 1140850688 | bytes 1572864 | tf_op jit(solution)/shard_map/sjk,jm->skm/dot_general | solution.py:40
  517.9 61.5 %fusion.33 = f32[2,64,2048]{2,1,0:T(8,128)S(1)} fusion(f32[2,64,2048]{2,1,0:T(8,128)S(1)} %fusion.12, bf16[2,4,2048,64]{2,3,0,1:T(8,128)(2,1)S(1)} %all_to_all.33), kind=kOutput, calls=%fused_computation.38 | convolution fusion | flops 1136918528 | bytes 2621440 | tf_op jit(solution)/shard_map/sjk,jm->skm/dot_general | solution.py:43
  579.4 61.9 %fusion.36 = f32[2,64,2048]{2,1,0:T(8,128)S(1)} fusion(f32[2,64,2048]{2,1,0:T(8,128)S(1)} %fusion.10, bf16[2,4,2048,64]{2,3,0,1:T(8,128)(2,1)S(1)} %all_to_all.33), kind=kOutput, calls=%fused_computation.39 | convolution fusion | flops 1136918528 | bytes 2621440 | tf_op jit(solution)/shard_map/sjk,jm->skm/dot_general | solution.py:38
  641.4 61.7 %fusion.30 = f32[2,64,2048]{2,1,0:T(8,128)S(1)} fusion(f32[2,64,2048]{2,1,0:T(8,128)S(1)} %fusion.14, bf16[2,4,2048,64]{2,3,0,1:T(8,128)(2,1)S(1)} %all_to_all.33), kind=kOutput, calls=%fused_computation.37 | convolution fusion | flops 1136918528 | bytes 2621440 | tf_op jit(solution)/shard_map/sjk,jm->skm/dot_general | solution.py:38
  703.1 61.9 %subtract_divide_fusion = f32[2,64,2048]{2,1,0:T(8,128)S(1)} fusion(f32[2,64,2048]{2,1,0:T(8,128)S(1)} %fusion.33, f32[2,64,2048]{2,1,0:T(8,128)S(1)} %fusion.30, f32[2,64,2048]{2,1,0:T(8,128)S(1)} %fusion.36, f32[2,64,2048]{2,1,0:T(8,128)S(1)} %fusion.8, f32[2]{0:T(128)S(1)} %subtract_multiply_fusion, f32[2]{0:T(128)S(1)} %get-tuple-element.21, ...), kind=kOutput, calls=%fused_computation.62 | convolution fusion | flops 1140850688 | bytes 5769216 | tf_op jit(solution)/shard_map/sjk,jm->skm/dot_general | solution.py:43
  765.8 9.0 %collective-permute-start.1 = (f32[2,8,2048]{2,1,0:T(8,128)S(1)}, f32[2,8,2048]{2,1,0:T(8,128)S(1)}, u32[]{:S(2)}, u32[]{:S(2)}) collective-permute-start(f32[2,8,2048]{2,1,0:T(8,128)S(1)} %get-tuple-element.48), channel_id=1, source_target_pairs={{1,0},{2,1},{3,2},{4,3},{5,4},{6,5},{7,6},{8,7},{9,8},{10,9},{11,1... | collective-permute-start | bytes 393224 | tf_op jit(solution)/shard_map/ppermute | solution.py:23
  778.0 2.5 broadcast.127.clone
  780.5 16.5 %while.2 = (s32[]{:T(128)}, f32[80,2048]{1,0:T(8,128)S(1)}, s32[8,2]{0,1:T(2,128)S(1)}, f32[8,64,2048]{2,1,0:T(8,128)}, s32[]{:T(128)}) while((s32[]{:T(128)}, f32[80,2048]{1,0:T(8,128)S(1)}, s32[8,2]{0,1:T(2,128)S(1)}, f32[8,64,2048]{2,1,0:T(8,128)}, s32[]{:T(128)}) %tuple.38), condition=%wide.while_cond, body=%wide.while_body.sunk | while | flops 2 | bytes 1049189 | solution.py:107
  799.5 16.6 %while.3 = (s32[]{:T(128)}, f32[80,2048]{1,0:T(8,128)S(1)}, s32[8,2]{0,1:T(2,128)S(1)}, f32[8,64,2048]{2,1,0:T(8,128)}, s32[]{:T(128)}) while((s32[]{:T(128)}, f32[80,2048]{1,0:T(8,128)S(1)}, s32[8,2]{0,1:T(2,128)S(1)}, f32[8,64,2048]{2,1,0:T(8,128)}, s32[]{:T(128)}) %tuple.41), condition=%wide.while_cond.1, body=%wide.while_body.1.sunk | while | flops 2 | bytes 1049189 | solution.py:107
  816.0 6.7 add_multiply_fusion
  (72 shorter events, 42.0 us)
Async XLA Ops:
  14.5 48.5 %all-to-all-start = ((bf16[16,2,32768]{2,1,0:T(2,128)(2,1)}), bf16[16,2,32768]{2,1,0:T(2,128)(2,1)S(1)}, u32[]{:S(2)}, u32[]{:S(2)}) async-start(bf16[16,2,32768]{2,1,0:T(2,128)(2,1)} %reshape.137), calls=%async_computation | async-start | bytes 4194304 | tf_op jit(solution)/shard_map/all_to_all | solution.py:82
  205.0 14.7 %copy-start = (f32[2,3]{1,0:T(2,128)S(1)}, f32[2,3]{1,0:T(2,128)}, u32[]{:S(2)}) copy-start(f32[2,3]{1,0:T(2,128)} %param.4) | copy-start | bytes 76
  208.5 52.3 %all-to-all-start.1 = ((bf16[2,4,128,1024]{2,0,1,3:T(2,128)(2,1)}), bf16[2,4,128,1024]{2,0,1,3:T(2,128)(2,1)S(1)}, u32[]{:S(2)}, u32[]{:S(2)}) async-start(bf16[2,4,128,1024]{2,0,1,3:T(2,128)(2,1)} %copy.8), calls=%async_computation.1 | async-start | bytes 4194304 | tf_op jit(solution)/shard_map/all_to_all | solution.py:91
  703.1 71.8 %copy-start.1 = (s32[8,2]{0,1:T(2,128)S(1)}, s32[8,2]{0,1:T(2,128)}, u32[]{:S(2)}) copy-start(s32[8,2]{0,1:T(2,128)} %param.5) | copy-start | bytes 196
  765.0 12.5 %collective-permute-start = (f32[2,8,2048]{2,1,0:T(8,128)S(1)}, f32[2,8,2048]{2,1,0:T(8,128)S(1)}, u32[]{:S(2)}, u32[]{:S(2)}) collective-permute-start(f32[2,8,2048]{2,1,0:T(8,128)S(1)} %get-tuple-element.47), channel_id=1, source_target_pairs={{0,1},{1,2},{2,3},{3,4},{4,5},{5,6},{6,7},{7,8},{8,9},{9,10},{10,1... | collective-permute-start | bytes 393224 | tf_op jit(solution)/shard_map/ppermute | solution.py:21
  765.8 11.6 %collective-permute-start.1 = (f32[2,8,2048]{2,1,0:T(8,128)S(1)}, f32[2,8,2048]{2,1,0:T(8,128)S(1)}, u32[]{:S(2)}, u32[]{:S(2)}) collective-permute-start(f32[2,8,2048]{2,1,0:T(8,128)S(1)} %get-tuple-element.48), channel_id=1, source_target_pairs={{1,0},{2,1},{3,2},{4,3},{5,4},{6,5},{7,6},{8,7},{9,8},{10,9},{11,1... | collective-permute-start | bytes 393224 | tf_op jit(solution)/shard_map/ppermute | solution.py:23
where the time goes:
time: 827 us; the launch traced here: 823 us
  matrix products  629 us (76%)
  waiting for transfers between devices  82.4 us (10%)
  local copies, waits for them, and re-layouts  72.7 us (9%)
  starting transfers between devices  28.5 us (3%)
  other arithmetic  9.56 us (1%)
    dot_general x4, matrix products, complex_dft(): jnp.einsum(formula, x_imag, w_imag, preferred_element_type=jnp.float32)  158 us
    dot_general x4, matrix products, complex_dft(): jnp.einsum(formula, x_real, w_imag, preferred_element_type=jnp.float32)  158 us
    dot_general x4, matrix products, complex_dft(): jnp.einsum(formula, x_imag, w_real, preferred_element_type=jnp.float32)  157 us
    dot_general x4, matrix products, complex_dft(): jnp.einsum(formula, x_real, w_real, preferred_element_type=jnp.float32)  156 us
    all_to_all x1, waiting for transfers between devices, local(): lax.all_to_all(twiddled, 'tm', split_axis=3, concat_axis=2, tiled=True)  40.9 us
    all_to_all x1, waiting for transfers between devices, local(): lax.all_to_all(series, 'tm', split_axis=3, concat_axis=2, tiled=True)  39 us
    gather x48, local copies, waits for them, and re-layouts  33 us
    unnamed x9, local copies, waits for them, and re-layouts  24.4 us
  transfers between devices with their start and end apart: 4, of which 3 were waited for; matrix products, arithmetic and copies ran while one was open for 0% of the time, Pallas kernels for 0%

commit v1 on v0

v1 whole, which is shorter than its diff:
```python
import functools
import math

import jax
import jax.numpy as jnp
import numpy as np
from jax import lax
from jax.experimental import pallas as pl
from jax.experimental.pallas import tpu as pltpu
from jax.sharding import PartitionSpec as P

DMAX = 8
LANES = 128
VMEM_LIMIT = 48 * 1024 * 1024
BF16 = jnp.bfloat16
F32 = jnp.float32


def params():
    return pltpu.CompilerParams(vmem_limit_bytes=VMEM_LIMIT)


def dft_table(length):
    indices = np.arange(length, dtype=np.int32)
    products = indices[:, None] * indices[None, :] % length
    angle = products.astype(np.float32) * np.float32(2.0 * math.pi / length)
    return np.cos(angle).astype(BF16), (-np.sin(angle)).astype(BF16)


def dot(x, y):
    return jnp.dot(x, y, preferred_element_type=F32)


def pack_kernel(x_ref, out_ref):
    cols = out_ref.shape[-1]
    for piece in range(out_ref.shape[0]):
        out_ref[piece] = x_ref[0, :, :, piece * cols : (piece + 1) * cols]


def pack(series, lead, groups):
    segs, _, rows, width = series.shape
    cols = width // groups
    return pl.pallas_call(
        pack_kernel,
        grid=(segs,),
        in_specs=[pl.BlockSpec((1, 2, rows, width), lambda s: (s, lead // 2, 0, 0))],
        out_specs=pl.BlockSpec((groups, 2, rows, cols), lambda s: (s, 0, 0, 0)),
        out_shape=jax.ShapeDtypeStruct((segs * groups, 2, rows, cols), BF16),
        compiler_params=params(),
        cost_estimate=pl.CostEstimate(flops=0, bytes_accessed=2 * 2 * 2 * segs * rows * width, transcendentals=0),
        name="pack",
    )(series)


def first_kernel(x_ref, wr_ref, wi_ref, tr_ref, ti_ref, out_ref):
    length = wr_ref.shape[1]
    cols = x_ref.shape[-1]
    x_real = x_ref[:, 0].reshape(length, cols)
    x_imag = x_ref[:, 1].reshape(length, cols)
    w_real, w_imag = wr_ref[...], wi_ref[...]
    real_part = dot(w_real, x_real) - dot(w_imag, x_imag)
    imag_part = dot(w_imag, x_real) + dot(w_real, x_imag)
    t_real, t_imag = tr_ref[...], ti_ref[...]
    shape = (out_ref.shape[0],) + out_ref.shape[3:]
    out_ref[:, 0, 0] = (real_part * t_real - imag_part * t_imag).astype(BF16).reshape(shape)
    out_ref[:, 1, 0] = (real_part * t_imag + imag_part * t_real).astype(BF16).reshape(shape)


def first_pass(pieces, tables, twiddles, groups):
    count, _, rows, cols = pieces.shape
    length = count * rows
    segs = count // groups
    per_seg = length // segs
    tile = min(256, per_seg)
    owners = tile // rows
    steps = per_seg // tile
    return pl.pallas_call(
        first_kernel,
        grid=(segs, steps),
        in_specs=[
            pl.BlockSpec((count, 2, rows, cols), lambda h, t: (0, 0, 0, 0)),
            pl.BlockSpec((tile, length), lambda h, t: (h * steps + t, 0)),
            pl.BlockSpec((tile, length), lambda h, t: (h * steps + t, 0)),
            pl.BlockSpec((tile, cols), lambda h, t: (h * steps + t, 0)),
            pl.BlockSpec((tile, cols), lambda h, t: (h * steps + t, 0)),
        ],
        out_specs=pl.BlockSpec((owners, 2, 1, rows, cols), lambda h, t: (t, 0, h, 0, 0)),
        out_shape=jax.ShapeDtypeStruct((groups, 2, segs, rows, cols), BF16),
        compiler_params=params(),
        cost_estimate=pl.CostEstimate(
            flops=8 * length * length * cols, bytes_accessed=4 * length * (length + 4 * cols), transcendentals=0
        ),
        name="first_pass",
    )(pieces, *tables, *twiddles)


def gather_rows(z_ref, lhs_ref):
    groups, _, _, _, cols = z_ref.shape
    for piece in range(groups):
        lhs_ref[:, piece * cols : (piece + 1) * cols] = z_ref[piece].reshape(lhs_ref.shape[0], cols)


def transform(lhs_ref, wr_ref, wi_ref):
    half = lhs_ref.shape[0] // 2
    by_real = dot(lhs_ref[...], wr_ref[...])
    by_imag = dot(lhs_ref[...], wi_ref[...])
    return by_real[:half] - by_imag[half:], by_imag[:half] + by_real[half:]


def second_kernel(z_ref, wr_ref, wi_ref, re_ref, im_ref, lhs_ref):
    @pl.when(pl.program_id(0) == 0)
    def _():
        gather_rows(z_ref, lhs_ref)

    re_ref[...], im_ref[...] = transform(lhs_ref, wr_ref, wi_ref)


def fstat_kernel(length, coef_ref, place_ref, z_ref, wr_ref, wi_ref, ar_ref, ai_ref, own_ref, other_ref, head_ref, tail_ref, lhs_ref):
    @pl.when(pl.program_id(0) == 0)
    def _():
        gather_rows(z_ref, lhs_ref)

    b_real, b_imag = transform(lhs_ref, wr_ref, wi_ref)
    a_real, a_imag = ar_ref[...], ai_ref[...]
    coef_a, coef_b, coef_c = coef_ref[0], coef_ref[1], coef_ref[2]
    numer = (
        coef_b * (a_real * a_real + a_imag * a_imag)
        + coef_a * (b_real * b_real + b_imag * b_imag)
        - 2.0 * coef_c * (a_real * b_real + a_imag * b_imag)
    )
    fstat = numer / ((coef_a * coef_b - coef_c * coef_c) * length)
    rows = own_ref.shape[0]
    first, last = fstat[:rows], fstat[rows:]
    is_first = place_ref[0] == 0
    own_ref[...] = jnp.where(is_first, first, last)
    other_ref[...] = jnp.where(is_first, last, first).astype(BF16)
    head_ref[...] = jnp.concatenate([first[:DMAX], last[:DMAX]], axis=0).astype(BF16)
    tail_ref[...] = jnp.concatenate([first[rows - DMAX :], last[rows - DMAX :]], axis=0).astype(BF16)


def second_specs(z, width, tile):
    return [
        pl.BlockSpec(z.shape, lambda t: (0, 0, 0, 0, 0)),
        pl.BlockSpec((width, tile), lambda t: (0, t)),
        pl.BlockSpec((width, tile), lambda t: (0, t)),
    ]


def second_pass(z, tables):
    groups, _, segs, rows, cols = z.shape
    width = groups * cols
    tile = 512
    height = segs * rows
    return pl.pallas_call(
        second_kernel,
        grid=(width // tile,),
        in_specs=second_specs(z, width, tile),
        out_specs=[pl.BlockSpec((height, tile), lambda t: (0, t))] * 2,
        out_shape=[jax.ShapeDtypeStruct((height, width), F32)] * 2,
        scratch_shapes=[pltpu.VMEM((2 * height, width), BF16)],
        compiler_params=params(),
        cost_estimate=pl.CostEstimate(
            flops=8 * height * width * width, bytes_accessed=4 * width * width, transcendentals=0
        ),
        name="second_pass",
    )(z, *tables)


def fstat_pass(z, tables, spectrum, coefs, place, length):
    groups, _, segs, rows, cols = z.shape
    width = groups * cols
    tile = 512
    height = segs * rows
    smem = pl.BlockSpec(memory_space=pltpu.SMEM)
    strip = lambda count: pl.BlockSpec((count, tile), lambda t: (0, t))
    return pl.pallas_call(
        functools.partial(fstat_kernel, length),
        grid=(width // tile,),
        in_specs=[smem, smem] + second_specs(z, width, tile) + [strip(height)] * 2,
        out_specs=[strip(rows), strip(rows), strip(segs * DMAX), strip(segs * DMAX)],
        out_shape=[
            jax.ShapeDtypeStruct((rows, width), F32),
            jax.ShapeDtypeStruct((rows, width), BF16),
            jax.ShapeDtypeStruct((segs * DMAX, width), BF16),
            jax.ShapeDtypeStruct((segs * DMAX, width), BF16),
        ],
        scratch_shapes=[pltpu.VMEM((2 * height, width), BF16)],
        compiler_params=params(),
        cost_estimate=pl.CostEstimate(
            flops=8 * height * width * width, bytes_accessed=4 * width * width, transcendentals=0
        ),
        name="fstat_pass",
    )(coefs, place, z, *tables, *spectrum)


def detect_kernel(offsets_ref, place_ref, own_ref, other_ref, own_rim_ref, other_rim_ref, out_ref, *wide_refs):
    rows = own_ref.shape[0]

    @pl.when(pl.program_id(0) == 0)
    def _():
        is_first, is_last, seg = place_ref[1] == 1, place_ref[2] == 1, place_ref[0]
        width = own_ref.shape[1]

        def widen(wide_ref, middle, rims):
            rims = rims.astype(F32)
            lower, upper = rims[:DMAX], rims[DMAX:]
            lower = jnp.where(is_first, pltpu.roll(lower, 1, 1), lower)
            upper = jnp.where(is_last, pltpu.roll(upper, width - 1, 1), upper)
            for strip in range(width // LANES):
                at = slice(strip * LANES, (strip + 1) * LANES)
                wide_ref[strip, :DMAX] = lower[:, at]
                wide_ref[strip, DMAX : DMAX + rows] = middle[:, at]
                wide_ref[strip, DMAX + rows :] = upper[:, at]

        def place(own_wide, other_wide):
            widen(own_wide, own_ref[...], own_rim_ref[...])
            widen(other_wide, other_ref[...].astype(F32), other_rim_ref[...])

        @pl.when(seg == 0)
        def _():
            place(wide_refs[0], wide_refs[1])

        @pl.when(seg != 0)
        def _():
            place(wide_refs[1], wide_refs[0])

    template = pl.program_id(0)
    begins = [DMAX + offsets_ref[template, s] for s in range(len(wide_refs))]
    for strip in range(own_ref.shape[1] // LANES):
        total = wide_refs[0][strip, pl.ds(begins[0], rows), :]
        for begin, wide_ref in zip(begins[1:], wide_refs[1:]):
            total = total + wide_ref[strip, pl.ds(begin, rows), :]
        out_ref[0, :, strip * LANES : (strip + 1) * LANES] = total / len(wide_refs)


def detect(offsets, place, own, other, own_rims, other_rims):
    templates = offsets.shape[0]
    rows, width = own.shape
    smem = pl.BlockSpec(memory_space=pltpu.SMEM)
    whole = lambda x: pl.BlockSpec(x.shape, lambda t: (0, 0))
    return pl.pallas_call(
        detect_kernel,
        grid=(templates,),
        in_specs=[smem, smem] + [whole(x) for x in (own, other, own_rims, other_rims)],
        out_specs=pl.BlockSpec((1, rows, width), lambda t: (t, 0, 0)),
        out_shape=jax.ShapeDtypeStruct((templates, rows, width), F32),
        scratch_shapes=[pltpu.VMEM((width // LANES, rows + 2 * DMAX, LANES), F32)] * 2,
        compiler_params=params(),
        cost_estimate=pl.CostEstimate(
            flops=3 * templates * rows * width, bytes_accessed=4 * templates * rows * width, transcendentals=0
        ),
        name="detect",
    )(offsets, place, own, other, own_rims, other_rims)


def local(series, antenna, offsets):
    devices = lax.axis_size("tm")
    index = lax.axis_index("tm")
    segs, _, rows, width = series.shape
    groups = devices // segs
    slow = devices * rows
    length = slow * width
    seg = index // groups
    member = index % groups
    cols = width // groups
    short = dft_table(slow)
    long = dft_table(width)

    halves = [[g * groups + i for i in range(groups)] for g in range(segs)]
    pieces = [pack(series, lead, groups) for lead in (0, 2)]
    pieces = [lax.all_to_all(x, "tm", split_axis=0, concat_axis=0, tiled=True) for x in pieces]

    columns = member * cols + jnp.arange(cols, dtype=jnp.int32)
    bins = jnp.arange(slow, dtype=jnp.int32)
    twist = (bins[:, None] * columns[None, :] % length).astype(F32) * (2.0 * math.pi / length)
    twiddles = (jnp.cos(twist), -jnp.sin(twist))

    turned = [first_pass(x, short, twiddles, groups) for x in pieces]
    turned = [
        lax.all_to_all(x, "tm", split_axis=0, concat_axis=0, axis_index_groups=halves, tiled=True) for x in turned
    ]
    spectrum = second_pass(turned[0], long)
    place = jnp.stack([seg, index == 0, index == devices - 1]).astype(jnp.int32)
    coefs = lax.dynamic_index_in_dim(antenna, seg, 0, keepdims=False)
    own, other, heads, tails = fstat_pass(turned[1], long, spectrum, coefs, place, length)

    swap = [(i, (i + groups) % devices) for i in range(devices)]
    other = lax.ppermute(other, "tm", swap)

    up = [(g * groups + i, g * groups + (i + 1) % groups) for g in range(segs) for i in range(groups)]
    down = [(target, source) for source, target in up]
    lower = lax.ppermute(tails, "tm", up).reshape(segs, DMAX, width)
    upper = lax.ppermute(heads, "tm", down).reshape(segs, DMAX, width)
    lower = jnp.where(member == 0, jnp.roll(lower, 1, axis=0), lower)
    upper = jnp.where(member == groups - 1, jnp.roll(upper, -1, axis=0), upper)
    rims = jnp.concatenate([lower, upper], axis=1)
    own_rims = lax.dynamic_index_in_dim(rims, seg, 0, keepdims=False)
    other_rims = lax.ppermute(lax.dynamic_index_in_dim(rims, 1 - seg, 0, keepdims=False), "tm", swap)
    return detect(offsets, place, own, other, own_rims, other_rims)


def solution(mesh):
    return jax.shard_map(
        local,
        mesh=mesh,
        in_specs=(P("sky", None, "tm", None), P("sky", None), P("sky", None)),
        out_specs=P("sky", "tm", None),
        check_vma=False,
    )
```

time: 827 us -> 137 us (0.17)
  matrix products: 629 us -> 0 us
  local copies, waits for them, and re-layouts: 72.7 us -> 9.29 us
  Pallas kernels: 0 us -> 33.7 us
  waiting for transfers between devices: 82.4 us -> 57.1 us
    dot_general x16 -> x0, matrix products: 629 us -> none  [the longest x4 158 us: complex_dft(): jnp.einsum(formula, x_imag, w_imag, preferred_element_type=jnp.float32)]
    all_to_all x2 -> x4, waiting for transfers between devices: 79.9 us -> 45.7 us  [the longest x2 33.7 us: local(): lax.all_to_all(x, 'tm', split_axis=0, concat_axis=0, tiled=True)]
    pallas_call x0 -> x7, Pallas kernels: none -> 33.7 us  [the longest x2 9.53 us: first_pass(): pl.pallas_call(first_kernel, grid=(segs, steps), in_specs=[pl.BlockSpec((...]
    gather x48 -> x0, local copies, waits for them, and re-layouts: 33 us -> none
    unnamed x9 -> x25, local copies, waits for them, and re-layouts: 24.4 us -> 9.27 us
    all_to_all x3 -> x0, local copies, waits for them, and re-layouts: 11.4 us -> none  [the longest x1 5.96 us: local(): lax.all_to_all(series, 'tm', split_axis=3, concat_axis=2, tiled=True)]
    ppermute x2 -> x4, waiting for transfers between devices: 2.49 us -> 11.4 us  [the longest x1 11.4 us: local(): lax.ppermute(lax.dynamic_index_in_dim(rims, 1 - seg, 0, keepdims=False),...]
    all_to_all x2 -> x4, starting transfers between devices: 18.6 us -> 23.7 us  [the longest x2 14.2 us: local(): lax.all_to_all(x, 'tm', split_axis=0, concat_axis=0, tiled=True)]
  transfers between devices with their start and end apart: 4 -> 8, of which waited for: 3 -> 5; matrix products, arithmetic and copies ran while one was open for 0% -> 3% of each run, Pallas kernels for 0% -> 14%
where the time goes in v1:
time: 137 us; the launch traced here: 136 us
  waiting for transfers between devices  57.1 us (42%)
  Pallas kernels  33.7 us (25%)
  starting transfers between devices  31.3 us (23%)
  local copies, waits for them, and re-layouts  9.29 us (7%)
  other arithmetic  4.26 us (3%)
    all_to_all x2, waiting for transfers between devices, local(): lax.all_to_all(x, 'tm', split_axis=0, concat_axis=0, tiled=True)  33.7 us
    all_to_all x2, starting transfers between devices, local(): lax.all_to_all(x, 'tm', split_axis=0, concat_axis=0, tiled=True)  14.2 us
    all_to_all x2, waiting for transfers between devices, local(): lax.all_to_all(x, 'tm', split_axis=0, concat_axis=0, axis_index_groups=ha...  12 us
    ppermute x1, waiting for transfers between devices, local(): lax.ppermute(lax.dynamic_index_in_dim(rims, 1 - seg, 0, keepdims=False),...  11.4 us
    pallas_call x2, Pallas kernels, first_pass(): pl.pallas_call(first_kernel, grid=(segs, steps), in_specs=[pl.BlockSpec((...  9.53 us
    all_to_all x2, starting transfers between devices, local(): lax.all_to_all(x, 'tm', split_axis=0, concat_axis=0, axis_index_groups=ha...  9.45 us
    unnamed x25, local copies, waits for them, and re-layouts  9.27 us
    pallas_call x1, Pallas kernels, fstat_pass(): pl.pallas_call(functools.partial(fstat_kernel, length), grid=(width // ti...  8.99 us
  transfers between devices with their start and end apart: 8, of which 5 were waited for; matrix products, arithmetic and copies ran while one was open for 3% of the time, Pallas kernels for 14%

profile of v1, /device:TPU:0, one launch (start us, length us, event | category | flops | bytes accessed | tf_op | source)
XLA Modules:
  0.0 135.9 jit_solution(12571074921111051228)
XLA Ops:
  0.0 1.6 %copy-done.1 = bf16[2,4,64,2048]{3,2,1,0:T(8,128)(2,1)S(1)} copy-done((bf16[2,4,64,2048]{3,2,1,0:T(8,128)(2,1)S(1)}, bf16[2,4,64,2048]{3,2,1,0:T(8,128)(2,1)}, u32[]{:S(2)}) %copy-start.1) | copy-done | bytes 2097176
  1.6 1.0 pack.3
  2.6 7.4 %all-to-all-start.2 = ((bf16[16,2,64,256]{3,2,1,0:T(8,128)(2,1)}), bf16[16,2,64,256]{3,2,1,0:T(8,128)(2,1)S(1)}, u32[]{:S(2)}, u32[]{:S(2)}) async-start(bf16[16,2,64,256]{3,2,1,0:T(8,128)(2,1)} %pack.3), calls=%async_computation.2 | async-start | bytes 2097152 | tf_op jit(solution)/shard_map/all_to_all | solution.py:271
  10.0 1.0 pack.2
  11.1 21.9 %all-to-all-done.2.x_ref = bf16[16,2,64,256]{3,2,1,0:T(8,128)(2,1)S(1)} async-done(((bf16[16,2,64,256]{3,2,1,0:T(8,128)(2,1)}), bf16[16,2,64,256]{3,2,1,0:T(8,128)(2,1)S(1)}, u32[]{:S(2)}, u32[]{:S(2)}) %all-to-all-start.2) | async-done | bytes 1048608 | tf_op jit(solution)/shard_map/all_to_all | solution.py:271
  33.0 6.9 %all-to-all-start = ((bf16[16,2,64,256]{3,2,1,0:T(8,128)(2,1)}), bf16[16,2,64,256]{3,2,1,0:T(8,128)(2,1)S(1)}, u32[]{:S(2)}, u32[]{:S(2)}) async-start(bf16[16,2,64,256]{3,2,1,0:T(8,128)(2,1)} %pack.2), calls=%async_computation | async-start | bytes 2097152 | tf_op jit(solution)/shard_map/all_to_all | solution.py:271
  39.9 4.1 %sine_negate_fusion = (f32[1024,256]{1,0:T(8,128)S(1)}, f32[1024,256]{1,0:T(8,128)S(1)}) fusion(s32[256]{0:T(256)S(1)} %iota_add_fusion), kind=kLoop, calls=%fused_computation.6 | loop fusion | flops 3932160 | bytes 2098176 | tf_op jit(solution)/shard_map/neg | solution.py:276
  44.0 1.2 copy-done.7
  45.2 4.8 %first_pass.3 = bf16[8,2,2,64,256]{4,3,2,1,0:T(8,128)(2,1)S(1)} custom-call(bf16[16,2,64,256]{3,2,1,0:T(8,128)(2,1)S(1)} %copy-done.7, bf16[1024,1024]{1,0:T(8,128)(2,1)} %constant.73.clone.wr_ref, bf16[1024,1024]{1,0:T(8,128)(2,1)} %constant.74.clone.wi_ref, f32[1024,256]{1,0:T(8,128)S(1)} %get-tuple-element.24.tr_ref, f32[1024,256]{1,0:T(8,128)S(1)} %get-tuple-element.23.ti_ref), custom_call_target="tpu_custom_call" | custom-call | flops 2147483648 | bytes 8388608 | tf_op jit(solution)/shard_map/first_pass/pallas_call | solution.py:77
  50.0 1.0 copy-done.8
  51.0 11.8 %all-to-all-done.x_ref = bf16[16,2,64,256]{3,2,1,0:T(8,128)(2,1)S(1)} async-done(((bf16[16,2,64,256]{3,2,1,0:T(8,128)(2,1)}), bf16[16,2,64,256]{3,2,1,0:T(8,128)(2,1)S(1)}, u32[]{:S(2)}, u32[]{:S(2)}) %all-to-all-start) | async-done | bytes 1048608 | tf_op jit(solution)/shard_map/all_to_all | solution.py:271
  62.8 1.0 copy-done.4
  63.8 5.9 %all-to-all-start.3 = ((bf16[8,2,2,64,256]{4,3,2,1,0:T(8,128)(2,1)}), bf16[8,2,2,64,256]{4,3,2,1,0:T(8,128)(2,1)S(1)}, u32[]{:S(2)}, u32[]{:S(2)}) async-start(bf16[8,2,2,64,256]{4,3,2,1,0:T(8,128)(2,1)} %copy-done.8), calls=%async_computation.3 | async-start | bytes 2097152 | tf_op jit(solution)/shard_map/all_to_all | solution.py:280
  69.7 1.2 copy-done.5
  70.9 4.8 %first_pass.2 = bf16[8,2,2,64,256]{4,3,2,1,0:T(8,128)(2,1)S(1)} custom-call(bf16[16,2,64,256]{3,2,1,0:T(8,128)(2,1)S(1)} %copy-done.5, bf16[1024,1024]{1,0:T(8,128)(2,1)} %constant.73.clone.wr_ref, bf16[1024,1024]{1,0:T(8,128)(2,1)} %constant.74.clone.wi_ref, f32[1024,256]{1,0:T(8,128)S(1)} %get-tuple-element.24.tr_ref, f32[1024,256]{1,0:T(8,128)S(1)} %get-tuple-element.23.ti_ref), custom_call_target="tpu_custom_call" | custom-call | flops 2147483648 | bytes 8388608 | tf_op jit(solution)/shard_map/first_pass/pallas_call | solution.py:77
  75.6 0.0 copy-start.3
  75.7 1.0 copy-done.3
  76.6 7.5 %all-to-all-done.3.z_ref = bf16[8,2,2,64,256]{4,3,2,1,0:T(8,128)(2,1)S(1)} async-done(((bf16[8,2,2,64,256]{4,3,2,1,0:T(8,128)(2,1)}), bf16[8,2,2,64,256]{4,3,2,1,0:T(8,128)(2,1)S(1)}, u32[]{:S(2)}, u32[]{:S(2)}) %all-to-all-start.3) | async-done | bytes 1048608 | tf_op jit(solution)/shard_map/all_to_all | solution.py:280
  84.1 3.6 %all-to-all-start.1 = ((bf16[8,2,2,64,256]{4,3,2,1,0:T(8,128)(2,1)}), bf16[8,2,2,64,256]{4,3,2,1,0:T(8,128)(2,1)S(1)}, u32[]{:S(2)}, u32[]{:S(2)}) async-start(bf16[8,2,2,64,256]{4,3,2,1,0:T(8,128)(2,1)} %copy-done.3), calls=%async_computation.1 | async-start | bytes 2097152 | tf_op jit(solution)/shard_map/all_to_all | solution.py:280
  87.7 0.1 pad_add_fusion.place_ref
  87.8 8.7 %second_pass.1 = (f32[128,2048]{1,0:T(8,128)S(1)}, f32[128,2048]{1,0:T(8,128)S(1)}) custom-call(bf16[8,2,2,64,256]{4,3,2,1,0:T(8,128)(2,1)S(1)} %all-to-all-done.3.z_ref, bf16[2048,2048]{1,0:T(8,128)(2,1)} %constant.75.clone.wr_ref, bf16[2048,2048]{1,0:T(8,128)(2,1)} %constant.76.clone.wi_ref), custom_call_target="tpu_custom_call" | custom-call | flops 4294967296 | bytes 16777216 | tf_op jit(solution)/shard_map/second_pass/pallas_call | solution.py:154
  96.5 1.0 copy-done.9
  97.5 4.6 %all-to-all-done.1.z_ref = bf16[8,2,2,64,256]{4,3,2,1,0:T(8,128)(2,1)S(1)} async-done(((bf16[8,2,2,64,256]{4,3,2,1,0:T(8,128)(2,1)}), bf16[8,2,2,64,256]{4,3,2,1,0:T(8,128)(2,1)S(1)}, u32[]{:S(2)}, u32[]{:S(2)}) %all-to-all-start.1) | async-done | bytes 1048608 | tf_op jit(solution)/shard_map/all_to_all | solution.py:280
  102.1 1.2 copy-done.10
  103.3 9.0 %fstat_pass.1 = (f32[64,2048]{1,0:T(8,128)S(1)}, bf16[64,2048]{1,0:T(8,128)(2,1)S(1)}, bf16[16,2048]{1,0:T(8,128)(2,1)S(1)}, bf16[16,2048]{1,0:T(8,128)(2,1)S(1)}) custom-call(f32[3]{0:T(128)S(1)} %fusion.11.coef_ref, s32[3]{0:T(128)S(1)} %pad_add_fusion.place_ref, bf16[8,2,2,64,256]{4,3,2,1,0:T(8,128)(2,1)S(1)} %all-to-all-done.1.z_ref, ...), custom_call_target="tpu_custom_call" | custom-call | flops 4294967296 | bytes 16777216 | tf_op jit(solution)/shard_map/fstat_pass/pallas_call | solution.py:176
  112.3 0.1 collective-permute-start.1
  112.4 2.6 %collective-permute-start.2 = (bf16[16,2048]{1,0:T(8,128)(2,1)S(1)}, bf16[16,2048]{1,0:T(8,128)(2,1)S(1)}, u32[]{:S(2)}, u32[]{:S(2)}) collective-permute-start(bf16[16,2048]{1,0:T(8,128)(2,1)S(1)} %get-tuple-element.16), channel_id=1, source_target_pairs={{1,0},{2,1},{3,2},{4,3},{5,4},{6,5},{7,6},{0,7},{9,8},{10,9},{11,1... | collective-permute-start | bytes 196616 | tf_op jit(solution)/shard_map/ppermute | solution.py:293
  115.0 2.7 %collective-permute-start = (bf16[64,2048]{1,0:T(8,128)(2,1)S(1)}, bf16[64,2048]{1,0:T(8,128)(2,1)S(1)}, u32[]{:S(2)}, u32[]{:S(2)}) collective-permute-start(bf16[64,2048]{1,0:T(8,128)(2,1)S(1)} %get-tuple-element.14), channel_id=1, source_target_pairs={{0,8},{1,9},{2,10},{3,11},{4,12},{5,13},{6,14},{7,15},{8,0},{9,1},... | collective-permute-start | bytes 786440 | tf_op jit(solution)/shard_map/ppermute | solution.py:288
  117.7 2.3 %collective-permute-start.3 = (bf16[16,2048]{1,0:T(8,128)(2,1)S(1)}, bf16[16,2048]{1,0:T(8,128)(2,1)S(1)}, u32[]{:S(2)}, u32[]{:S(2)}) collective-permute-start(bf16[16,2048]{1,0:T(8,128)(2,1)S(1)} %get-tuple-element.17), channel_id=1, source_target_pairs={{0,8},{1,9},{2,10},{3,11},{4,12},{5,13},{6,14},{7,15},{8,0},{9,1},... | collective-permute-start | bytes 196616 | tf_op jit(solution)/shard_map/ppermute | solution.py:298
  120.0 0.1 copy.8.offsets_ref
  120.1 11.4 %collective-permute-done.3.other_rim_ref = bf16[16,2048]{1,0:T(8,128)(2,1)S(1)} collective-permute-done((bf16[16,2048]{1,0:T(8,128)(2,1)S(1)}, bf16[16,2048]{1,0:T(8,128)(2,1)S(1)}, u32[]{:S(2)}, u32[]{:S(2)}) %collective-permute-start.3) | collective-permute-done | bytes 65568 | tf_op jit(solution)/shard_map/ppermute | solution.py:298
  131.5 4.4 %detect.1 = f32[8,64,2048]{2,1,0:T(8,128)} custom-call(s32[8,2]{1,0:T(8,128)S(1)} %copy.8.offsets_ref, s32[3]{0:T(128)S(1)} %pad_add_fusion.place_ref, f32[64,2048]{1,0:T(8,128)S(1)} %get-tuple-element.13.own_ref, bf16[64,2048]{1,0:T(8,128)(2,1)S(1)} %collective-permute-done.other_ref, bf16[16,2048]{1,0:T(8,128)(2,1)S(1)} %get-tuple-element.18.own_rim_ref, ...), custom_call_target="tpu_custom_call" | custom-call | flops 3145728 | bytes 4194304 | tf_op jit(solution)/shard_map/detect/pallas_call | solution.py:241
  (25 shorter events, 0.1 us)
Async XLA Ops:
  0.0 87.7 %copy-start = (f32[2,3]{1,0:T(2,128)S(1)}, f32[2,3]{1,0:T(2,128)}, u32[]{:S(2)}) copy-start(f32[2,3]{1,0:T(2,128)} %param.8) | copy-start | bytes 76
  0.0 1.6 %copy-start.1 = (bf16[2,4,64,2048]{3,2,1,0:T(8,128)(2,1)S(1)}, bf16[2,4,64,2048]{3,2,1,0:T(8,128)(2,1)}, u32[]{:S(2)}) copy-start(bf16[2,4,64,2048]{3,2,1,0:T(8,128)(2,1)} %x_ref.3) | copy-start | bytes 6291460
  1.6 8.4 %copy-start.2 = (bf16[2,4,64,2048]{3,2,1,0:T(8,128)(2,1)S(1)}, bf16[2,4,64,2048]{3,2,1,0:T(8,128)(2,1)}, u32[]{:S(2)}) copy-start(bf16[2,4,64,2048]{3,2,1,0:T(8,128)(2,1)} %x_ref.3) | copy-start | bytes 6291460
  2.6 30.3 %all-to-all-start.2 = ((bf16[16,2,64,256]{3,2,1,0:T(8,128)(2,1)}), bf16[16,2,64,256]{3,2,1,0:T(8,128)(2,1)S(1)}, u32[]{:S(2)}, u32[]{:S(2)}) async-start(bf16[16,2,64,256]{3,2,1,0:T(8,128)(2,1)} %pack.3), calls=%async_computation.2 | async-start | bytes 2097152 | tf_op jit(solution)/shard_map/all_to_all | solution.py:271
  33.0 6.9 %copy-start.6 = (bf16[16,2,64,256]{3,2,1,0:T(8,128)(2,1)}, bf16[16,2,64,256]{3,2,1,0:T(8,128)(2,1)S(1)}, u32[]{:S(2)}) copy-start(bf16[16,2,64,256]{3,2,1,0:T(8,128)(2,1)S(1)} %all-to-all-done.2.x_ref) | copy-start | bytes 3145732
  33.0 29.8 %all-to-all-start = ((bf16[16,2,64,256]{3,2,1,0:T(8,128)(2,1)}), bf16[16,2,64,256]{3,2,1,0:T(8,128)(2,1)S(1)}, u32[]{:S(2)}, u32[]{:S(2)}) async-start(bf16[16,2,64,256]{3,2,1,0:T(8,128)(2,1)} %pack.2), calls=%async_computation | async-start | bytes 2097152 | tf_op jit(solution)/shard_map/all_to_all | solution.py:271
  44.0 1.2 copy-start.7
  50.0 1.0 copy-start.8
  62.8 1.0 copy-start.4
  63.8 20.4 %all-to-all-start.3 = ((bf16[8,2,2,64,256]{4,3,2,1,0:T(8,128)(2,1)}), bf16[8,2,2,64,256]{4,3,2,1,0:T(8,128)(2,1)S(1)}, u32[]{:S(2)}, u32[]{:S(2)}) async-start(bf16[8,2,2,64,256]{4,3,2,1,0:T(8,128)(2,1)} %copy-done.8), calls=%async_computation.3 | async-start | bytes 2097152 | tf_op jit(solution)/shard_map/all_to_all | solution.py:280
  69.7 1.2 copy-start.5
  75.6 1.0 copy-start.3
  84.1 17.9 %all-to-all-start.1 = ((bf16[8,2,2,64,256]{4,3,2,1,0:T(8,128)(2,1)}), bf16[8,2,2,64,256]{4,3,2,1,0:T(8,128)(2,1)S(1)}, u32[]{:S(2)}, u32[]{:S(2)}) async-start(bf16[8,2,2,64,256]{4,3,2,1,0:T(8,128)(2,1)} %copy-done.3), calls=%async_computation.1 | async-start | bytes 2097152 | tf_op jit(solution)/shard_map/all_to_all | solution.py:280
  96.5 1.0 copy-start.9
  102.1 1.2 copy-start.10
  103.3 16.7 %copy-start.11 = (s32[8,2]{0,1:T(2,128)S(1)}, s32[8,2]{0,1:T(2,128)}, u32[]{:S(2)}) copy-start(s32[8,2]{0,1:T(2,128)} %param.9) | copy-start | bytes 196
  112.3 5.4 %collective-permute-start.1 = (bf16[16,2048]{1,0:T(8,128)(2,1)S(1)}, bf16[16,2048]{1,0:T(8,128)(2,1)S(1)}, u32[]{:S(2)}, u32[]{:S(2)}) collective-permute-start(bf16[16,2048]{1,0:T(8,128)(2,1)S(1)} %get-tuple-element.15), channel_id=1, source_target_pairs={{0,1},{1,2},{2,3},{3,4},{4,5},{5,6},{6,7},{7,0},{8,9},{9,10},{10,1... | collective-permute-start | bytes 196616 | tf_op jit(solution)/shard_map/ppermute | solution.py:292
  112.4 5.3 %collective-permute-start.2 = (bf16[16,2048]{1,0:T(8,128)(2,1)S(1)}, bf16[16,2048]{1,0:T(8,128)(2,1)S(1)}, u32[]{:S(2)}, u32[]{:S(2)}) collective-permute-start(bf16[16,2048]{1,0:T(8,128)(2,1)S(1)} %get-tuple-element.16), channel_id=1, source_target_pairs={{1,0},{2,1},{3,2},{4,3},{5,4},{6,5},{7,6},{0,7},{9,8},{10,9},{11,1... | collective-permute-start | bytes 196616 | tf_op jit(solution)/shard_map/ppermute | solution.py:293
  115.0 16.5 %collective-permute-start = (bf16[64,2048]{1,0:T(8,128)(2,1)S(1)}, bf16[64,2048]{1,0:T(8,128)(2,1)S(1)}, u32[]{:S(2)}, u32[]{:S(2)}) collective-permute-start(bf16[64,2048]{1,0:T(8,128)(2,1)S(1)} %get-tuple-element.14), channel_id=1, source_target_pairs={{0,8},{1,9},{2,10},{3,11},{4,12},{5,13},{6,14},{7,15},{8,0},{9,1},... | collective-permute-start | bytes 786440 | tf_op jit(solution)/shard_map/ppermute | solution.py:288
  117.7 13.7 %collective-permute-start.3 = (bf16[16,2048]{1,0:T(8,128)(2,1)S(1)}, bf16[16,2048]{1,0:T(8,128)(2,1)S(1)}, u32[]{:S(2)}, u32[]{:S(2)}) collective-permute-start(bf16[16,2048]{1,0:T(8,128)(2,1)S(1)} %get-tuple-element.17), channel_id=1, source_target_pairs={{0,8},{1,9},{2,10},{3,11},{4,12},{5,13},{6,14},{7,15},{8,0},{9,1},... | collective-permute-start | bytes 196616 | tf_op jit(solution)/shard_map/ppermute | solution.py:298

commit v2 on v1

v2 whole, which is shorter than its diff:
```python
import functools
import math

import jax
import jax.numpy as jnp
import numpy as np
from jax import lax
from jax.experimental import pallas as pl
from jax.experimental.pallas import tpu as pltpu
from jax.sharding import PartitionSpec as P

DMAX = 8
LANES = 128
DEVICE, CHIP, MEMBER, SEG, FIRST, LAST = range(6)
BF16 = jnp.bfloat16
F32 = jnp.float32


SMEM = pl.BlockSpec(memory_space=pltpu.SMEM)
VMEM = pl.BlockSpec(memory_space=pltpu.VMEM)


def params(mebibytes):
    return pltpu.CompilerParams(vmem_limit_bytes=mebibytes * 1024 * 1024)


def dft_table(length):
    indices = np.arange(length, dtype=np.int32)
    products = indices[:, None] * indices[None, :] % length
    angle = products.astype(np.float32) * np.float32(2.0 * math.pi / length)
    return np.cos(angle).astype(BF16), (-np.sin(angle)).astype(BF16)


def dot(x, y):
    return jnp.dot(x, y, preferred_element_type=F32)


def pack_kernel(lead, place_ref, x_ref, *refs):
    out_refs, sem = refs[:-1], refs[-1]
    cols = out_refs[0].shape[-1]
    groups = x_ref.shape[-1] // cols
    copies = []
    for turn, out_ref in enumerate(out_refs):
        chip = place_ref[CHIP] ^ turn
        begin = pl.multiple_of(chip % groups * cols, cols)
        source = x_ref.at[chip // groups, pl.ds(lead, 2), :, pl.ds(begin, cols)]
        copies.append(pltpu.make_async_copy(source, out_ref, sem.at[turn]))
        copies[-1].start()
    for copy in copies:
        copy.wait()


def pack(series, place, lead, chips):
    segs, _, rows, width = series.shape
    cols = width * segs // chips
    return pl.pallas_call(
        functools.partial(pack_kernel, lead),
        in_specs=[SMEM, pl.BlockSpec(memory_space=pl.ANY)],
        out_specs=[VMEM] * chips,
        out_shape=[jax.ShapeDtypeStruct((2, rows, cols), BF16)] * chips,
        scratch_shapes=[pltpu.SemaphoreType.DMA((chips,))],
        compiler_params=params(16),
        cost_estimate=pl.CostEstimate(flops=0, bytes_accessed=8 * segs * rows * width, transcendentals=0),
        name="pack",
    )(place, series)


def first_kernel(chips, groups, place_ref, *refs):
    piece_refs, refs = refs[: 2 * chips], refs[2 * chips :]
    wr_ref, wi_ref, tr_ref, ti_ref = refs[:4]
    out_refs, x_ref = refs[4:-1], refs[-1]
    rows = piece_refs[0].shape[1]
    for turn in range(2 * chips):
        source = place_ref[DEVICE] ^ turn
        x_ref[:, pl.ds(pl.multiple_of(source * rows, rows), rows), :] = piece_refs[turn][...]
    height = out_refs[0].shape[1]
    cols = x_ref.shape[-1]
    tile = min(256, cols)
    for begin in range(0, cols, tile):
        at = slice(begin, begin + tile)
        x_real, x_imag = x_ref[0, :, at], x_ref[1, :, at]
        w_real, w_imag = wr_ref[...], wi_ref[...]
        real_part = dot(w_real, x_real) - dot(w_imag, x_imag)
        imag_part = dot(w_imag, x_real) + dot(w_real, x_imag)
        t_real, t_imag = tr_ref[:, at], ti_ref[:, at]
        turned_real = (real_part * t_real - imag_part * t_imag).astype(BF16)
        turned_imag = (real_part * t_imag + imag_part * t_real).astype(BF16)
        for turn, out_ref in enumerate(out_refs):
            part = slice(turn * height, (turn + 1) * height)
            out_ref[0, :, at] = turned_real[part]
            out_ref[1, :, at] = turned_imag[part]


def first_pass(pieces, place, tables, twiddles, groups):
    chips = len(pieces) // 2
    _, rows, cols = pieces[0].shape
    length = 2 * chips * rows
    height = length // 2 // groups
    return pl.pallas_call(
        functools.partial(first_kernel, chips, groups),
        in_specs=[SMEM] + [VMEM] * (len(pieces) + 4),
        out_specs=[VMEM] * groups,
        out_shape=[jax.ShapeDtypeStruct((2, height, cols), BF16)] * groups,
        scratch_shapes=[pltpu.VMEM((2, length, cols), BF16)],
        compiler_params=params(16),
        cost_estimate=pl.CostEstimate(
            flops=4 * length * length * cols, bytes_accessed=2 * length * length, transcendentals=0
        ),
        name="first_pass",
    )(place, *pieces, *tables, *twiddles)


def gather_rows(place_ref, piece_refs, lhs_ref):
    @pl.when(pl.program_id(0) == 0)
    def _():
        cols = piece_refs[0].shape[-1]
        for turn, piece_ref in enumerate(piece_refs):
            begin = pl.multiple_of((place_ref[MEMBER] ^ turn) * cols, cols)
            lhs_ref[:, pl.ds(begin, cols)] = piece_ref[...].reshape(lhs_ref.shape[0], cols)


def transform(lhs_ref, wr_ref, wi_ref):
    half = lhs_ref.shape[0] // 2
    by_real = dot(lhs_ref[...], wr_ref[...])
    by_imag = dot(lhs_ref[...], wi_ref[...])
    return by_real[:half] - by_imag[half:], by_imag[:half] + by_real[half:]


def second_kernel(groups, place_ref, *refs):
    wr_ref, wi_ref, re_ref, im_ref, lhs_ref = refs[groups:]
    gather_rows(place_ref, refs[:groups], lhs_ref)
    re_ref[...], im_ref[...] = transform(lhs_ref, wr_ref, wi_ref)


def fstat_kernel(groups, length, place_ref, coef_ref, *refs):
    wr_ref, wi_ref, ar_ref, ai_ref, own_ref, other_ref, head_ref, tail_ref, lhs_ref = refs[groups:]
    gather_rows(place_ref, refs[:groups], lhs_ref)
    b_real, b_imag = transform(lhs_ref, wr_ref, wi_ref)
    a_real, a_imag = ar_ref[...], ai_ref[...]
    coef_a, coef_b, coef_c = coef_ref[0], coef_ref[1], coef_ref[2]
    numer = (
        coef_b * (a_real * a_real + a_imag * a_imag)
        + coef_a * (b_real * b_real + b_imag * b_imag)
        - 2.0 * coef_c * (a_real * b_real + a_imag * b_imag)
    )
    fstat = numer / ((coef_a * coef_b - coef_c * coef_c) * length)
    rows = own_ref.shape[0]
    first, last = fstat[:rows], fstat[rows:]
    is_first = place_ref[SEG] == 0
    own_ref[...] = jnp.where(is_first, first, last)
    other_ref[...] = jnp.where(is_first, last, first).astype(BF16)
    head_ref[...] = jnp.concatenate([first[:DMAX], last[:DMAX]], axis=0).astype(BF16)
    tail_ref[...] = jnp.concatenate([first[rows - DMAX :], last[rows - DMAX :]], axis=0).astype(BF16)


def second_specs(pieces, width, tile):
    return [pl.BlockSpec(x.shape, lambda t: (0, 0, 0)) for x in pieces] + [
        pl.BlockSpec((width, tile), lambda t: (0, t)),
        pl.BlockSpec((width, tile), lambda t: (0, t)),
    ]


def second_pass(pieces, place, tables):
    groups = len(pieces)
    _, height, cols = pieces[0].shape
    width = groups * cols
    tile = 512
    return pl.pallas_call(
        functools.partial(second_kernel, groups),
        grid=(width // tile,),
        in_specs=[SMEM] + second_specs(pieces, width, tile),
        out_specs=[pl.BlockSpec((height, tile), lambda t: (0, t))] * 2,
        out_shape=[jax.ShapeDtypeStruct((height, width), F32)] * 2,
        scratch_shapes=[pltpu.VMEM((2 * height, width), BF16)],
        compiler_params=params(24),
        cost_estimate=pl.CostEstimate(
            flops=8 * height * width * width, bytes_accessed=4 * width * width, transcendentals=0
        ),
        name="second_pass",
    )(place, *pieces, *tables)


def fstat_pass(pieces, place, tables, spectrum, coefs, rows, length):
    groups = len(pieces)
    _, height, cols = pieces[0].shape
    width = groups * cols
    tile = 512
    rims = height // rows * DMAX
    strip = lambda count: pl.BlockSpec((count, tile), lambda t: (0, t))
    return pl.pallas_call(
        functools.partial(fstat_kernel, groups, length),
        grid=(width // tile,),
        in_specs=[SMEM, SMEM] + second_specs(pieces, width, tile) + [strip(height)] * 2,
        out_specs=[strip(rows), strip(rows), strip(rims), strip(rims)],
        out_shape=[
            jax.ShapeDtypeStruct((rows, width), F32),
            jax.ShapeDtypeStruct((rows, width), BF16),
            jax.ShapeDtypeStruct((rims, width), BF16),
            jax.ShapeDtypeStruct((rims, width), BF16),
        ],
        scratch_shapes=[pltpu.VMEM((2 * height, width), BF16)],
        compiler_params=params(24),
        cost_estimate=pl.CostEstimate(
            flops=8 * height * width * width, bytes_accessed=4 * width * width, transcendentals=0
        ),
        name="fstat_pass",
    )(place, coefs, *pieces, *tables, *spectrum)


def detect_kernel(offsets_ref, place_ref, own_ref, other_ref, own_rim_ref, other_rim_ref, out_ref, *wide_refs):
    rows = own_ref.shape[0]

    @pl.when(pl.program_id(0) == 0)
    def _():
        is_first, is_last, seg = place_ref[FIRST] == 1, place_ref[LAST] == 1, place_ref[SEG]
        width = own_ref.shape[1]

        def widen(wide_ref, middle, rims):
            rims = rims.astype(F32)
            lower, upper = rims[:DMAX], rims[DMAX:]
            lower = jnp.where(is_first, pltpu.roll(lower, 1, 1), lower)
            upper = jnp.where(is_last, pltpu.roll(upper, width - 1, 1), upper)
            for strip in range(width // LANES):
                at = slice(strip * LANES, (strip + 1) * LANES)
                wide_ref[strip, :DMAX] = lower[:, at]
                wide_ref[strip, DMAX : DMAX + rows] = middle[:, at]
                wide_ref[strip, DMAX + rows :] = upper[:, at]

        def place(own_wide, other_wide):
            widen(own_wide, own_ref[...], own_rim_ref[...])
            widen(other_wide, other_ref[...].astype(F32), other_rim_ref[...])

        @pl.when(seg == 0)
        def _():
            place(wide_refs[0], wide_refs[1])

        @pl.when(seg != 0)
        def _():
            place(wide_refs[1], wide_refs[0])

    template = pl.program_id(0)
    begins = [DMAX + offsets_ref[template, s] for s in range(len(wide_refs))]
    for strip in range(own_ref.shape[1] // LANES):
        total = wide_refs[0][strip, pl.ds(begins[0], rows), :]
        for begin, wide_ref in zip(begins[1:], wide_refs[1:]):
            total = total + wide_ref[strip, pl.ds(begin, rows), :]
        out_ref[0, :, strip * LANES : (strip + 1) * LANES] = total / len(wide_refs)


def detect(offsets, place, own, other, own_rims, other_rims):
    templates = offsets.shape[0]
    rows, width = own.shape
    whole = lambda x: pl.BlockSpec(x.shape, lambda t: (0, 0))
    return pl.pallas_call(
        detect_kernel,
        grid=(templates,),
        in_specs=[SMEM, SMEM] + [whole(x) for x in (own, other, own_rims, other_rims)],
        out_specs=pl.BlockSpec((1, rows, width), lambda t: (t, 0, 0)),
        out_shape=jax.ShapeDtypeStruct((templates, rows, width), F32),
        scratch_shapes=[pltpu.VMEM((width // LANES, rows + 2 * DMAX, LANES), F32)] * 2,
        compiler_params=params(16),
        cost_estimate=pl.CostEstimate(
            flops=3 * templates * rows * width, bytes_accessed=4 * templates * rows * width, transcendentals=0
        ),
        name="detect",
    )(offsets, place, own, other, own_rims, other_rims)


def trade(pieces, step, devices):
    return [pieces[0]] + [
        lax.ppermute(x, "tm", [(i, i ^ (turn * step)) for i in range(devices)])
        for turn, x in enumerate(pieces)
        if turn
    ]


def share(pieces, devices):
    pairs = [(i, i ^ 1) for i in range(devices)]
    return [y for x in pieces for y in (x, lax.ppermute(x, "tm", pairs))]


def local(series, antenna, offsets):
    devices = lax.axis_size("tm")
    index = lax.axis_index("tm")
    segs, _, rows, width = series.shape
    slow = devices * rows
    length = slow * width
    chips = devices // 2
    groups = chips // segs
    cols = width // groups
    core, chip = index % 2, index // 2
    seg, member = chip // groups, chip % groups
    short = dft_table(slow)
    long = dft_table(width)
    place = jnp.stack([index, chip, member, seg, index == 0, index == devices - 1]).astype(jnp.int32)

    received = [trade(pack(series, place, lead, chips), 2, devices) for lead in (0, 2)]
    received = [share(pieces, devices) for pieces in received]

    def owned(table):
        table = table.reshape((segs, groups, 2, rows) + table.shape[1:])
        table = lax.dynamic_index_in_dim(table, core, 2, keepdims=False)
        parts = [lax.dynamic_index_in_dim(table, member ^ turn, 1, keepdims=False) for turn in range(groups)]
        return jnp.stack(parts).reshape((slow // 2,) + table.shape[3:])

    columns = member * cols + jnp.arange(cols, dtype=jnp.int32)
    bins = owned(jnp.arange(slow, dtype=jnp.int32))
    twist = (bins[:, None] * columns[None, :] % length).astype(F32) * (2.0 * math.pi / length)
    twiddles = (jnp.cos(twist), -jnp.sin(twist))
    short = [owned(jnp.asarray(x)) for x in short]

    turned = [trade(first_pass(x, place, short, twiddles, groups), 2, devices) for x in received]
    spectrum = second_pass(turned[0], place, long)
    coefs = lax.dynamic_index_in_dim(antenna, seg, 0, keepdims=False)
    own, other, heads, tails = fstat_pass(turned[1], place, long, spectrum, coefs, rows, length)

    members = 2 * groups
    swap = [(i, (i + members) % devices) for i in range(devices)]
    other = lax.ppermute(other, "tm", swap)

    up = [(g * members + i, g * members + (i + 1) % members) for g in range(segs) for i in range(members)]
    down = [(target, source) for source, target in up]
    lower = lax.ppermute(tails, "tm", up).reshape(segs, DMAX, width)
    upper = lax.ppermute(heads, "tm", down).reshape(segs, DMAX, width)
    lower = jnp.where(index % members == 0, jnp.roll(lower, 1, axis=0), lower)
    upper = jnp.where(index % members == members - 1, jnp.roll(upper, -1, axis=0), upper)
    rims = jnp.concatenate([lower, upper], axis=1)
    own_rims = lax.dynamic_index_in_dim(rims, seg, 0, keepdims=False)
    other_rims = lax.ppermute(lax.dynamic_index_in_dim(rims, 1 - seg, 0, keepdims=False), "tm", swap)
    return detect(offsets, place, own, other, own_rims, other_rims)


def solution(mesh):
    return jax.shard_map(
        local,
        mesh=mesh,
        in_specs=(P("sky", None, "tm", None), P("sky", None), P("sky", None)),
        out_specs=P("sky", "tm", None),
        check_vma=False,
    )
```

time: 137 us -> 125 us (0.912)
  waiting for transfers between devices: 57.1 us -> 40.2 us
  starting transfers between devices: 31.3 us -> 43 us
  Pallas kernels: 33.7 us -> 28.5 us
    all_to_all x4 -> x0, waiting for transfers between devices: 45.7 us -> none  [the longest x2 33.7 us: local(): lax.all_to_all(x, 'tm', split_axis=0, concat_axis=0, tiled=True)]
    ppermute x0 -> x36, starting transfers between devices: none -> 37.9 us  [the longest x20 34.5 us: trade(): lax.ppermute(x, 'tm', [(i, i ^ turn * step) for i in range(devices)])]
    ppermute x0 -> x36, waiting for transfers between devices: none -> 26.9 us  [the longest x20 26.5 us: trade(): lax.ppermute(x, 'tm', [(i, i ^ turn * step) for i in range(devices)])]
    all_to_all x4 -> x0, starting transfers between devices: 23.7 us -> none  [the longest x2 14.2 us: local(): lax.all_to_all(x, 'tm', split_axis=0, concat_axis=0, tiled=True)]
    ppermute x1, waiting for transfers between devices: 0.01 us -> 5.28 us  [local(): upper = lax.ppermute(heads, 'tm', down).reshape(segs, DMAX, width)]
    pallas_call x7, Pallas kernels: 33.7 us -> 28.5 us  [the longest x1 7.28 us: fstat_pass(): pl.pallas_call(functools.partial(fstat_kernel, groups, length), grid=(wid...]
    ppermute x1, waiting for transfers between devices: 11.4 us -> 8.08 us  [local(): lax.ppermute(lax.dynamic_index_in_dim(rims, 1 - seg, 0, keepdims=False),...]
    unnamed x25 -> x31, local copies, waits for them, and re-layouts: 9.27 us -> 6.22 us
  transfers between devices with their start and end apart: 8 -> 40, of which waited for: 5 -> 8; matrix products, arithmetic and copies ran while one was open for 3% -> 5% of each run, Pallas kernels for 14% -> 12%
where the time goes in v2:
time: 125 us
  starting transfers between devices  43 us (34%)
  waiting for transfers between devices  40.2 us (32%)
  Pallas kernels  28.5 us (23%)
  local copies, waits for them, and re-layouts  8.13 us (7%)
  other arithmetic  4.51 us (4%)
    ppermute x20, starting transfers between devices, trade(): lax.ppermute(x, 'tm', [(i, i ^ turn * step) for i in range(devices)])  34.5 us
    ppermute x20, waiting for transfers between devices, trade(): lax.ppermute(x, 'tm', [(i, i ^ turn * step) for i in range(devices)])  26.5 us
    ppermute x1, waiting for transfers between devices, local(): lax.ppermute(lax.dynamic_index_in_dim(rims, 1 - seg, 0, keepdims=False),...  8.08 us
    pallas_call x1, Pallas kernels, fstat_pass(): pl.pallas_call(functools.partial(fstat_kernel, groups, length), grid=(wid...  7.28 us
    pallas_call x2, Pallas kernels, first_pass(): pl.pallas_call(functools.partial(first_kernel, chips, groups), in_specs=[...  7.12 us
    pallas_call x1, Pallas kernels, second_pass(): pl.pallas_call(functools.partial(second_kernel, groups), grid=(width // t...  7.03 us
    unnamed x31, local copies, waits for them, and re-layouts  6.22 us
    ppermute x1, waiting for transfers between devices, local(): upper = lax.ppermute(heads, 'tm', down).reshape(segs, DMAX, width)  5.28 us
  transfers between devices with their start and end apart: 40, of which 8 were waited for; matrix products, arithmetic and copies ran while one was open for 5% of the time, Pallas kernels for 12%

profile of v2, /device:TPU:0, one launch (start us, length us, event | category | flops | bytes accessed | tf_op | source)
XLA Modules:
  0.0 124.6 jit_solution(289584715327457848)
XLA Ops:
  0.1 1.6 %copy-done.2 = bf16[2,4,64,2048]{3,2,1,0:T(8,128)(2,1)S(1)} copy-done((bf16[2,4,64,2048]{3,2,1,0:T(8,128)(2,1)S(1)}, bf16[2,4,64,2048]{3,2,1,0:T(8,128)(2,1)}, u32[]{:S(2)}) %copy-start.2) | copy-done | bytes 2097176
  1.7 1.8 %pack.2 = (bf16[2,64,512]{2,1,0:T(8,128)(2,1)S(1)}, bf16[2,64,512]{2,1,0:T(8,128)(2,1)}, bf16[2,64,512]{2,1,0:T(8,128)(2,1)}, bf16[2,64,512]{2,1,0:T(8,128)(2,1)...) custom-call(s32[6]{0:T(128)S(1)} %stack.80.place_ref, ...), custom_call_target="tpu_custom_call" | custom-call | bytes 2097152 | tf_op jit(solution)/shard_map/pack/pallas_call | solution.py:56
  4.0 2.6 %collective-permute-start.1 = (bf16[2,64,512]{2,1,0:T(8,128)(2,1)}, bf16[2,64,512]{2,1,0:T(8,128)(2,1)S(1)}, u32[]{:S(2)}, u32[]{:S(2)}) collective-permute-start(bf16[2,64,512]{2,1,0:T(8,128)(2,1)} %get-tuple-element.36), channel_id=1, source_target_pairs={{0,2},{1,3},{2,0},{3,1},{4,6},{5,7},{6,4},{7,5},{8,10},{9,11},{10,... | collective-permute-start | bytes 393224 | tf_op jit(solution)/shard_map/ppermute | solution.py:271
  6.6 1.6 %collective-permute-start.3 = (bf16[2,64,512]{2,1,0:T(8,128)(2,1)}, bf16[2,64,512]{2,1,0:T(8,128)(2,1)S(1)}, u32[]{:S(2)}, u32[]{:S(2)}) collective-permute-start(bf16[2,64,512]{2,1,0:T(8,128)(2,1)} %get-tuple-element.37), channel_id=1, source_target_pairs={{0,4},{1,5},{2,6},{3,7},{4,0},{5,1},{6,2},{7,3},{8,12},{9,13},{10,... | collective-permute-start | bytes 393224 | tf_op jit(solution)/shard_map/ppermute | solution.py:271
  8.1 3.0 %collective-permute-start.7 = (bf16[2,64,512]{2,1,0:T(8,128)(2,1)}, bf16[2,64,512]{2,1,0:T(8,128)(2,1)S(1)}, u32[]{:S(2)}, u32[]{:S(2)}) collective-permute-start(bf16[2,64,512]{2,1,0:T(8,128)(2,1)} %get-tuple-element.39), channel_id=1, source_target_pairs={{0,8},{1,9},{2,10},{3,11},{4,12},{5,13},{6,14},{7,15},{8,0},{9,1},... | collective-permute-start | bytes 393224 | tf_op jit(solution)/shard_map/ppermute | solution.py:271
  16.7 1.3 %collective-permute-start.9 = (bf16[2,64,512]{2,1,0:T(8,128)(2,1)}, bf16[2,64,512]{2,1,0:T(8,128)(2,1)S(1)}, u32[]{:S(2)}, u32[]{:S(2)}) collective-permute-start(bf16[2,64,512]{2,1,0:T(8,128)(2,1)} %get-tuple-element.40), channel_id=1, source_target_pairs={{0,10},{1,11},{2,8},{3,9},{4,14},{5,15},{6,12},{7,13},{8,2},{9,3},... | collective-permute-start | bytes 393224 | tf_op jit(solution)/shard_map/ppermute | solution.py:271
  18.0 3.6 %collective-permute-start.11 = (bf16[2,64,512]{2,1,0:T(8,128)(2,1)}, bf16[2,64,512]{2,1,0:T(8,128)(2,1)S(1)}, u32[]{:S(2)}, u32[]{:S(2)}) collective-permute-start(bf16[2,64,512]{2,1,0:T(8,128)(2,1)} %get-tuple-element.41), channel_id=1, source_target_pairs={{0,12},{1,13},{2,14},{3,15},{4,8},{5,9},{6,10},{7,11},{8,4},{9,5},... | collective-permute-start | bytes 393224 | tf_op jit(solution)/shard_map/ppermute | solution.py:271
  21.7 1.7 %collective-permute-start.19 = (bf16[2,64,512]{2,1,0:T(8,128)(2,1)}, bf16[2,64,512]{2,1,0:T(8,128)(2,1)}, u32[]{:S(2)}, u32[]{:S(2)}) collective-permute-start(bf16[2,64,512]{2,1,0:T(8,128)(2,1)} %copy-done.11), channel_id=1, source_target_pairs={{0,2},{1,3},{2,0},{3,1},{4,6},{5,7},{6,4},{7,5},{8,10},{9,11},{10,... | collective-permute-start | bytes 393224 | tf_op jit(solution)/shard_map/ppermute | solution.py:271
  23.3 4.2 %sine_negate_fusion = (f32[512,512]{1,0:T(8,128)S(1)}, f32[512,512]{1,0:T(8,128)S(1)}) fusion(s32[512]{0:T(512)S(1)} %iota_add_fusion, s32[512]{0:T(512)S(1)} %mul.24), kind=kLoop, calls=%fused_computation.10 | loop fusion | flops 3932160 | bytes 2101248 | tf_op jit(solution)/shard_map/neg | solution.py:309
  27.5 5.5 %collective-permute-done.9.refs_10_ = bf16[2,64,512]{2,1,0:T(8,128)(2,1)S(1)} collective-permute-done((bf16[2,64,512]{2,1,0:T(8,128)(2,1)}, bf16[2,64,512]{2,1,0:T(8,128)(2,1)S(1)}, u32[]{:S(2)}, u32[]{:S(2)}) %collective-permute-start.9) | collective-permute-done | bytes 131104 | tf_op jit(solution)/shard_map/ppermute | solution.py:271
  33.0 3.4 %collective-permute-start.23 = (bf16[2,64,512]{2,1,0:T(8,128)(2,1)}, bf16[2,64,512]{2,1,0:T(8,128)(2,1)S(1)}, u32[]{:S(2)}, u32[]{:S(2)}) collective-permute-start(bf16[2,64,512]{2,1,0:T(8,128)(2,1)} %copy-done.9), channel_id=1, source_target_pairs={{0,6},{1,7},{2,4},{3,5},{4,2},{5,3},{6,0},{7,1},{8,14},{9,15},{10,... | collective-permute-start | bytes 393224 | tf_op jit(solution)/shard_map/ppermute | solution.py:271
  36.4 1.6 %collective-permute-start.25 = (bf16[2,64,512]{2,1,0:T(8,128)(2,1)}, bf16[2,64,512]{2,1,0:T(8,128)(2,1)S(1)}, u32[]{:S(2)}, u32[]{:S(2)}) collective-permute-start(bf16[2,64,512]{2,1,0:T(8,128)(2,1)} %copy-done.8), channel_id=1, source_target_pairs={{0,8},{1,9},{2,10},{3,11},{4,12},{5,13},{6,14},{7,15},{8,0},{9,1},... | collective-permute-start | bytes 393224 | tf_op jit(solution)/shard_map/ppermute | solution.py:271
  38.0 2.3 %collective-permute-start.27 = (bf16[2,64,512]{2,1,0:T(8,128)(2,1)}, bf16[2,64,512]{2,1,0:T(8,128)(2,1)S(1)}, u32[]{:S(2)}, u32[]{:S(2)}) collective-permute-start(bf16[2,64,512]{2,1,0:T(8,128)(2,1)} %copy-done.7), channel_id=1, source_target_pairs={{0,10},{1,11},{2,8},{3,9},{4,14},{5,15},{6,12},{7,13},{8,2},{9,3},... | collective-permute-start | bytes 393224 | tf_op jit(solution)/shard_map/ppermute | solution.py:271
  40.3 1.6 %collective-permute-start.29 = (bf16[2,64,512]{2,1,0:T(8,128)(2,1)}, bf16[2,64,512]{2,1,0:T(8,128)(2,1)S(1)}, u32[]{:S(2)}, u32[]{:S(2)}) collective-permute-start(bf16[2,64,512]{2,1,0:T(8,128)(2,1)} %copy-done.6), channel_id=1, source_target_pairs={{0,12},{1,13},{2,14},{3,15},{4,8},{5,9},{6,10},{7,11},{8,4},{9,5},... | collective-permute-start | bytes 393224 | tf_op jit(solution)/shard_map/ppermute | solution.py:271
  41.9 1.7 %dynamic-slice_bitcast_fusion.3 = (bf16[1,2,64,1024]{3,2,1,0:T(8,128)(2,1)S(1)}, bf16[1,2,64,1024]{3,2,1,0:T(8,128)(2,1)S(1)}, bf16[1,2,64,1024]{3,2,1,0:T(8,128...) fusion(bf16[2,4,2,64,1024]{4,3,0,2,1:T(8,128)(2,1)} %constant.4, ...), kind=kLoop, calls=%fused_computation.15 | loop fusion | bytes 4194324 | tf_op jit(solution)/shard_map/stack | solution.py:304
  43.7 2.2 %collective-permute-start.31 = (bf16[2,64,512]{2,1,0:T(8,128)(2,1)S(1)}, bf16[2,64,512]{2,1,0:T(8,128)(2,1)S(1)}, u32[]{:S(2)}, u32[]{:S(2)}) collective-permute-start(bf16[2,64,512]{2,1,0:T(8,128)(2,1)S(1)} %copy-done.5), channel_id=1, source_target_pairs={{0,14},{1,15},{2,12},{3,13},{4,10},{5,11},{6,8},{7,9},{8,6},{9,7},... | collective-permute-start | bytes 393224 | tf_op jit(solution)/shard_map/ppermute | solution.py:271
  45.9 8.6 %collective-permute-done.25.refs_8_ = bf16[2,64,512]{2,1,0:T(8,128)(2,1)S(1)} collective-permute-done((bf16[2,64,512]{2,1,0:T(8,128)(2,1)}, bf16[2,64,512]{2,1,0:T(8,128)(2,1)S(1)}, u32[]{:S(2)}, u32[]{:S(2)}) %collective-permute-start.25) | collective-permute-done | bytes 131104 | tf_op jit(solution)/shard_map/ppermute | solution.py:271
  54.5 3.5 %collective-permute-done.27.refs_10_ = bf16[2,64,512]{2,1,0:T(8,128)(2,1)S(1)} collective-permute-done((bf16[2,64,512]{2,1,0:T(8,128)(2,1)}, bf16[2,64,512]{2,1,0:T(8,128)(2,1)S(1)}, u32[]{:S(2)}, u32[]{:S(2)}) %collective-permute-start.27) | collective-permute-done | bytes 131104 | tf_op jit(solution)/shard_map/ppermute | solution.py:271
  61.6 4.0 %first_pass.3 = (bf16[2,128,512]{2,1,0:T(8,128)(2,1)S(1)}, bf16[2,128,512]{2,1,0:T(8,128)(2,1)S(1)}, bf16[2,128,512]{2,1,0:T(8,128)(2,1)S(1)}, bf16[2,128,512]{2,1,0:T(8,128)(2,1)S(1)}) custom-call(s32[6]{0:T(128)S(1)} %stack.80.place_ref, bf16[2,64,512]{2,1,0:T(8,128)(2,1)S(1)} %get-tuple-element.47.refs_0_, ...), custom_call_target="tpu_custom_call" | custom-call | flops 2147483648 | bytes 2097152 | tf_op jit(solution)/shard_map/first_pass/pallas_call | solution.py:99
  66.5 4.2 %collective-permute-start.34 = (bf16[2,128,512]{2,1,0:T(8,128)(2,1)S(1)}, bf16[2,128,512]{2,1,0:T(8,128)(2,1)S(1)}, u32[]{:S(2)}, u32[]{:S(2)}) collective-permute-start(bf16[2,128,512]{2,1,0:T(8,128)(2,1)S(1)} %get-tuple-element.57), channel_id=1, source_target_pairs={{0,4},{1,5},{2,6},{3,7},{4,0},{5,1},{6,2},{7,3},{8,12},{9,13},{10,... | collective-permute-start | bytes 786440 | tf_op jit(solution)/shard_map/ppermute | solution.py:271
  71.4 3.1 %first_pass.2 = (bf16[2,128,512]{2,1,0:T(8,128)(2,1)S(1)}, bf16[2,128,512]{2,1,0:T(8,128)(2,1)S(1)}, bf16[2,128,512]{2,1,0:T(8,128)(2,1)S(1)}, bf16[2,128,512]{2,1,0:T(8,128)(2,1)S(1)}) custom-call(s32[6]{0:T(128)S(1)} %stack.80.place_ref, bf16[2,64,512]{2,1,0:T(8,128)(2,1)S(1)} %get-tuple-element.35.refs_0_, ...), custom_call_target="tpu_custom_call" | custom-call | flops 2147483648 | bytes 2097152 | tf_op jit(solution)/shard_map/first_pass/pallas_call | solution.py:99
  75.5 2.0 %collective-permute-start.16 = (bf16[2,128,512]{2,1,0:T(8,128)(2,1)S(1)}, bf16[2,128,512]{2,1,0:T(8,128)(2,1)S(1)}, u32[]{:S(2)}, u32[]{:S(2)}) collective-permute-start(bf16[2,128,512]{2,1,0:T(8,128)(2,1)S(1)} %get-tuple-element.45), channel_id=1, source_target_pairs={{0,4},{1,5},{2,6},{3,7},{4,0},{5,1},{6,2},{7,3},{8,12},{9,13},{10,... | collective-permute-start | bytes 786440 | tf_op jit(solution)/shard_map/ppermute | solution.py:271
  77.4 1.0 collective-permute-start.17
  78.5 5.6 %collective-permute-done.35.refs_3_ = bf16[2,128,512]{2,1,0:T(8,128)(2,1)S(1)} collective-permute-done((bf16[2,128,512]{2,1,0:T(8,128)(2,1)S(1)}, bf16[2,128,512]{2,1,0:T(8,128)(2,1)S(1)}, u32[]{:S(2)}, u32[]{:S(2)}) %collective-permute-start.35) | collective-permute-done | bytes 262176 | tf_op jit(solution)/shard_map/ppermute | solution.py:271
  84.1 7.0 %second_pass.1 = (f32[128,2048]{1,0:T(8,128)S(1)}, f32[128,2048]{1,0:T(8,128)S(1)}) custom-call(s32[6]{0:T(128)S(1)} %stack.80.place_ref, bf16[2,128,512]{2,1,0:T(8,128)(2,1)S(1)} %get-tuple-element.55.refs_0_, bf16[2,128,512]{2,1,0:T(8,128)(2,1)S(1)} %collective-permute-done.33.refs_1_, bf16[2,128,512]{2,1,0:T(8,128)(2,1)S(1)} %collective-permute-done.34.refs_2_, ...), custom_call_target="tpu_custom_call" | custom-call | flops 4294967296 | bytes 16777216 | tf_op jit(solution)/shard_map/second_pass/pallas_call | solution.py:168
  91.2 3.2 %collective-permute-done.17.refs_3_ = bf16[2,128,512]{2,1,0:T(8,128)(2,1)S(1)} collective-permute-done((bf16[2,128,512]{2,1,0:T(8,128)(2,1)S(1)}, bf16[2,128,512]{2,1,0:T(8,128)(2,1)S(1)}, u32[]{:S(2)}, u32[]{:S(2)}) %collective-permute-start.17) | collective-permute-done | bytes 262176 | tf_op jit(solution)/shard_map/ppermute | solution.py:271
  94.3 7.3 %fstat_pass.1 = (f32[64,2048]{1,0:T(8,128)S(1)}, bf16[64,2048]{1,0:T(8,128)(2,1)S(1)}, bf16[16,2048]{1,0:T(8,128)(2,1)S(1)}, bf16[16,2048]{1,0:T(8,128)(2,1)S(1)}) custom-call(s32[6]{0:T(128)S(1)} %stack.80.place_ref, f32[3]{0:T(128)S(1)} %fusion.12.coef_ref, bf16[2,128,512]{2,1,0:T(8,128)(2,1)S(1)} %get-tuple-element.43.refs_0_, ...), custom_call_target="tpu_custom_call" | custom-call | flops 4294967296 | bytes 16777216 | tf_op jit(solution)/shard_map/fstat_pass/pallas_call | solution.py:190
  101.7 2.6 %collective-permute-start.36 = (bf16[64,2048]{1,0:T(8,128)(2,1)S(1)}, bf16[64,2048]{1,0:T(8,128)(2,1)S(1)}, u32[]{:S(2)}, u32[]{:S(2)}) collective-permute-start(bf16[64,2048]{1,0:T(8,128)(2,1)S(1)} %get-tuple-element.62), channel_id=1, source_target_pairs={{0,8},{1,9},{2,10},{3,11},{4,12},{5,13},{6,14},{7,15},{8,0},{9,1},... | collective-permute-start | bytes 786440 | tf_op jit(solution)/shard_map/ppermute | solution.py:319
  104.4 2.2 %collective-permute-start.38 = (bf16[16,2048]{1,0:T(8,128)(2,1)S(1)}, bf16[16,2048]{1,0:T(8,128)(2,1)S(1)}, u32[]{:S(2)}, u32[]{:S(2)}) collective-permute-start(bf16[16,2048]{1,0:T(8,128)(2,1)S(1)} %get-tuple-element.64), channel_id=1, source_target_pairs={{1,0},{2,1},{3,2},{4,3},{5,4},{6,5},{7,6},{0,7},{9,8},{10,9},{11,1... | collective-permute-start | bytes 196616 | tf_op jit(solution)/shard_map/ppermute | solution.py:324
  106.6 5.3 %collective-permute-done.38 = bf16[16,2048]{1,0:T(8,128)(2,1)S(1)} collective-permute-done((bf16[16,2048]{1,0:T(8,128)(2,1)S(1)}, bf16[16,2048]{1,0:T(8,128)(2,1)S(1)}, u32[]{:S(2)}, u32[]{:S(2)}) %collective-permute-start.38) | collective-permute-done | bytes 65568 | tf_op jit(solution)/shard_map/ppermute | solution.py:324
  112.1 8.1 %collective-permute-done.39.other_rim_ref = bf16[16,2048]{1,0:T(8,128)(2,1)S(1)} collective-permute-done((bf16[16,2048]{1,0:T(8,128)(2,1)S(1)}, bf16[16,2048]{1,0:T(8,128)(2,1)S(1)}, u32[]{:S(2)}, u32[]{:S(2)}) %collective-permute-start.39) | collective-permute-done | bytes 65568 | tf_op jit(solution)/shard_map/ppermute | solution.py:329
  120.2 4.4 %detect.1 = f32[8,64,2048]{2,1,0:T(8,128)} custom-call(s32[8,2]{1,0:T(8,128)S(1)} %copy.8.offsets_ref, s32[6]{0:T(128)S(1)} %stack.80.place_ref, f32[64,2048]{1,0:T(8,128)S(1)} %get-tuple-element.61.own_ref, bf16[64,2048]{1,0:T(8,128)(2,1)S(1)} %collective-permute-done.36.other_ref, bf16[16,2048]{1,0:T(8,128)(2,1)S(1)} %get-tuple-element.74.own_rim_ref, ...), custom_call_target="tpu_custom_call" | custom-call | flops 3145728 | bytes 4194304 | tf_op jit(solution)/shard_map/detect/pallas_call | solution.py:254
  (103 shorter events, 12.5 us)
Async XLA Ops:
  3.4 13.2 %collective-permute-start = (bf16[2,64,512]{2,1,0:T(8,128)(2,1)S(1)}, bf16[2,64,512]{2,1,0:T(8,128)(2,1)S(1)}, u32[]{:S(2)}, u32[]{:S(2)}) collective-permute-start(bf16[2,64,512]{2,1,0:T(8,128)(2,1)S(1)} %get-tuple-element.35.refs_0_), channel_id=1, source_target_pairs={{0,1},{1,0},{2,3},{3,2},{4,5},{5,4},{6,7},{7,6},{8,9},{9,8},{10,11... | collective-permute-start | bytes 393224 | tf_op jit(solution)/shard_map/ppermute | solution.py:279
  4.0 14.0 %collective-permute-start.1 = (bf16[2,64,512]{2,1,0:T(8,128)(2,1)}, bf16[2,64,512]{2,1,0:T(8,128)(2,1)S(1)}, u32[]{:S(2)}, u32[]{:S(2)}) collective-permute-start(bf16[2,64,512]{2,1,0:T(8,128)(2,1)} %get-tuple-element.36), channel_id=1, source_target_pairs={{0,2},{1,3},{2,0},{3,1},{4,6},{5,7},{6,4},{7,5},{8,10},{9,11},{10,... | collective-permute-start | bytes 393224 | tf_op jit(solution)/shard_map/ppermute | solution.py:271
  6.6 15.0 %collective-permute-start.3 = (bf16[2,64,512]{2,1,0:T(8,128)(2,1)}, bf16[2,64,512]{2,1,0:T(8,128)(2,1)S(1)}, u32[]{:S(2)}, u32[]{:S(2)}) collective-permute-start(bf16[2,64,512]{2,1,0:T(8,128)(2,1)} %get-tuple-element.37), channel_id=1, source_target_pairs={{0,4},{1,5},{2,6},{3,7},{4,0},{5,1},{6,2},{7,3},{8,12},{9,13},{10,... | collective-permute-start | bytes 393224 | tf_op jit(solution)/shard_map/ppermute | solution.py:271
  8.1 13.5 %collective-permute-start.5 = (bf16[2,64,512]{2,1,0:T(8,128)(2,1)S(1)}, bf16[2,64,512]{2,1,0:T(8,128)(2,1)S(1)}, u32[]{:S(2)}, u32[]{:S(2)}) collective-permute-start(bf16[2,64,512]{2,1,0:T(8,128)(2,1)S(1)} %get-tuple-element.38), channel_id=1, source_target_pairs={{0,6},{1,7},{2,4},{3,5},{4,2},{5,3},{6,0},{7,1},{8,14},{9,15},{10,... | collective-permute-start | bytes 393224 | tf_op jit(solution)/shard_map/ppermute | solution.py:271
  8.1 13.5 %collective-permute-start.7 = (bf16[2,64,512]{2,1,0:T(8,128)(2,1)}, bf16[2,64,512]{2,1,0:T(8,128)(2,1)S(1)}, u32[]{:S(2)}, u32[]{:S(2)}) collective-permute-start(bf16[2,64,512]{2,1,0:T(8,128)(2,1)} %get-tuple-element.39), channel_id=1, source_target_pairs={{0,8},{1,9},{2,10},{3,11},{4,12},{5,13},{6,14},{7,15},{8,0},{9,1},... | collective-permute-start | bytes 393224 | tf_op jit(solution)/shard_map/ppermute | solution.py:271
  16.7 16.4 %collective-permute-start.9 = (bf16[2,64,512]{2,1,0:T(8,128)(2,1)}, bf16[2,64,512]{2,1,0:T(8,128)(2,1)S(1)}, u32[]{:S(2)}, u32[]{:S(2)}) collective-permute-start(bf16[2,64,512]{2,1,0:T(8,128)(2,1)} %get-tuple-element.40), channel_id=1, source_target_pairs={{0,10},{1,11},{2,8},{3,9},{4,14},{5,15},{6,12},{7,13},{8,2},{9,3},... | collective-permute-start | bytes 393224 | tf_op jit(solution)/shard_map/ppermute | solution.py:271
  18.0 15.0 %collective-permute-start.11 = (bf16[2,64,512]{2,1,0:T(8,128)(2,1)}, bf16[2,64,512]{2,1,0:T(8,128)(2,1)S(1)}, u32[]{:S(2)}, u32[]{:S(2)}) collective-permute-start(bf16[2,64,512]{2,1,0:T(8,128)(2,1)} %get-tuple-element.41), channel_id=1, source_target_pairs={{0,12},{1,13},{2,14},{3,15},{4,8},{5,9},{6,10},{7,11},{8,4},{9,5},... | collective-permute-start | bytes 393224 | tf_op jit(solution)/shard_map/ppermute | solution.py:271
  21.6 14.8 %collective-permute-start.13 = (bf16[2,64,512]{2,1,0:T(8,128)(2,1)}, bf16[2,64,512]{2,1,0:T(8,128)(2,1)S(1)}, u32[]{:S(2)}, u32[]{:S(2)}) collective-permute-start(bf16[2,64,512]{2,1,0:T(8,128)(2,1)} %get-tuple-element.42), channel_id=1, source_target_pairs={{0,14},{1,15},{2,12},{3,13},{4,10},{5,11},{6,8},{7,9},{8,6},{9,7},... | collective-permute-start | bytes 393224 | tf_op jit(solution)/shard_map/ppermute | solution.py:271
  21.6 16.4 %collective-permute-start.18 = (bf16[2,64,512]{2,1,0:T(8,128)(2,1)S(1)}, bf16[2,64,512]{2,1,0:T(8,128)(2,1)S(1)}, u32[]{:S(2)}, u32[]{:S(2)}) collective-permute-start(bf16[2,64,512]{2,1,0:T(8,128)(2,1)S(1)} %get-tuple-element.47.refs_0_), channel_id=1, source_target_pairs={{0,1},{1,0},{2,3},{3,2},{4,5},{5,4},{6,7},{7,6},{8,9},{9,8},{10,11... | collective-permute-start | bytes 393224 | tf_op jit(solution)/shard_map/ppermute | solution.py:279
  21.7 18.6 %collective-permute-start.19 = (bf16[2,64,512]{2,1,0:T(8,128)(2,1)}, bf16[2,64,512]{2,1,0:T(8,128)(2,1)}, u32[]{:S(2)}, u32[]{:S(2)}) collective-permute-start(bf16[2,64,512]{2,1,0:T(8,128)(2,1)} %copy-done.11), channel_id=1, source_target_pairs={{0,2},{1,3},{2,0},{3,1},{4,6},{5,7},{6,4},{7,5},{8,10},{9,11},{10,... | collective-permute-start | bytes 393224 | tf_op jit(solution)/shard_map/ppermute | solution.py:271
  33.0 10.7 %collective-permute-start.21 = (bf16[2,64,512]{2,1,0:T(8,128)(2,1)}, bf16[2,64,512]{2,1,0:T(8,128)(2,1)S(1)}, u32[]{:S(2)}, u32[]{:S(2)}) collective-permute-start(bf16[2,64,512]{2,1,0:T(8,128)(2,1)} %copy-done.10), channel_id=1, source_target_pairs={{0,4},{1,5},{2,6},{3,7},{4,0},{5,1},{6,2},{7,3},{8,12},{9,13},{10,... | collective-permute-start | bytes 393224 | tf_op jit(solution)/shard_map/ppermute | solution.py:271
  33.0 12.9 %collective-permute-start.23 = (bf16[2,64,512]{2,1,0:T(8,128)(2,1)}, bf16[2,64,512]{2,1,0:T(8,128)(2,1)S(1)}, u32[]{:S(2)}, u32[]{:S(2)}) collective-permute-start(bf16[2,64,512]{2,1,0:T(8,128)(2,1)} %copy-done.9), channel_id=1, source_target_pairs={{0,6},{1,7},{2,4},{3,5},{4,2},{5,3},{6,0},{7,1},{8,14},{9,15},{10,... | collective-permute-start | bytes 393224 | tf_op jit(solution)/shard_map/ppermute | solution.py:271
  36.4 18.1 %collective-permute-start.25 = (bf16[2,64,512]{2,1,0:T(8,128)(2,1)}, bf16[2,64,512]{2,1,0:T(8,128)(2,1)S(1)}, u32[]{:S(2)}, u32[]{:S(2)}) collective-permute-start(bf16[2,64,512]{2,1,0:T(8,128)(2,1)} %copy-done.8), channel_id=1, source_target_pairs={{0,8},{1,9},{2,10},{3,11},{4,12},{5,13},{6,14},{7,15},{8,0},{9,1},... | collective-permute-start | bytes 393224 | tf_op jit(solution)/shard_map/ppermute | solution.py:271
  38.0 20.1 %collective-permute-start.27 = (bf16[2,64,512]{2,1,0:T(8,128)(2,1)}, bf16[2,64,512]{2,1,0:T(8,128)(2,1)S(1)}, u32[]{:S(2)}, u32[]{:S(2)}) collective-permute-start(bf16[2,64,512]{2,1,0:T(8,128)(2,1)} %copy-done.7), channel_id=1, source_target_pairs={{0,10},{1,11},{2,8},{3,9},{4,14},{5,15},{6,12},{7,13},{8,2},{9,3},... | collective-permute-start | bytes 393224 | tf_op jit(solution)/shard_map/ppermute | solution.py:271
  40.3 17.8 %collective-permute-start.29 = (bf16[2,64,512]{2,1,0:T(8,128)(2,1)}, bf16[2,64,512]{2,1,0:T(8,128)(2,1)S(1)}, u32[]{:S(2)}, u32[]{:S(2)}) collective-permute-start(bf16[2,64,512]{2,1,0:T(8,128)(2,1)} %copy-done.6), channel_id=1, source_target_pairs={{0,12},{1,13},{2,14},{3,15},{4,8},{5,9},{6,10},{7,11},{8,4},{9,5},... | collective-permute-start | bytes 393224 | tf_op jit(solution)/shard_map/ppermute | solution.py:271
  43.7 15.0 %collective-permute-start.31 = (bf16[2,64,512]{2,1,0:T(8,128)(2,1)S(1)}, bf16[2,64,512]{2,1,0:T(8,128)(2,1)S(1)}, u32[]{:S(2)}, u32[]{:S(2)}) collective-permute-start(bf16[2,64,512]{2,1,0:T(8,128)(2,1)S(1)} %copy-done.5), channel_id=1, source_target_pairs={{0,14},{1,15},{2,12},{3,13},{4,10},{5,11},{6,8},{7,9},{8,6},{9,7},... | collective-permute-start | bytes 393224 | tf_op jit(solution)/shard_map/ppermute | solution.py:271
  45.9 12.9 %collective-permute-start.2 = (bf16[2,64,512]{2,1,0:T(8,128)(2,1)S(1)}, bf16[2,64,512]{2,1,0:T(8,128)(2,1)S(1)}, u32[]{:S(2)}, u32[]{:S(2)}) collective-permute-start(bf16[2,64,512]{2,1,0:T(8,128)(2,1)S(1)} %collective-permute-done.1.refs_2_), channel_id=1, source_target_pairs={{0,1},{1,0},{2,3},{3,2},{4,5},{5,4},{6,7},{7,6},{8,9},{9,8},{10,11... | collective-permute-start | bytes 393224 | tf_op jit(solution)/shard_map/ppermute | solution.py:279
  60.4 5.3 %collective-permute-start.6 = (bf16[2,64,512]{2,1,0:T(8,128)(2,1)S(1)}, bf16[2,64,512]{2,1,0:T(8,128)(2,1)S(1)}, u32[]{:S(2)}, u32[]{:S(2)}) collective-permute-start(bf16[2,64,512]{2,1,0:T(8,128)(2,1)S(1)} %collective-permute-done.5.refs_6_), channel_id=1, source_target_pairs={{0,1},{1,0},{2,3},{3,2},{4,5},{5,4},{6,7},{7,6},{8,9},{9,8},{10,11... | collective-permute-start | bytes 393224 | tf_op jit(solution)/shard_map/ppermute | solution.py:279
  60.6 5.9 %collective-permute-start.8 = (bf16[2,64,512]{2,1,0:T(8,128)(2,1)S(1)}, bf16[2,64,512]{2,1,0:T(8,128)(2,1)S(1)}, u32[]{:S(2)}, u32[]{:S(2)}) collective-permute-start(bf16[2,64,512]{2,1,0:T(8,128)(2,1)S(1)} %collective-permute-done.7.refs_8_), channel_id=1, source_target_pairs={{0,1},{1,0},{2,3},{3,2},{4,5},{5,4},{6,7},{7,6},{8,9},{9,8},{10,11... | collective-permute-start | bytes 393224 | tf_op jit(solution)/shard_map/ppermute | solution.py:279
  61.0 9.7 %collective-permute-start.10 = (bf16[2,64,512]{2,1,0:T(8,128)(2,1)S(1)}, bf16[2,64,512]{2,1,0:T(8,128)(2,1)S(1)}, u32[]{:S(2)}, u32[]{:S(2)}) collective-permute-start(bf16[2,64,512]{2,1,0:T(8,128)(2,1)S(1)} %collective-permute-done.9.refs_10_), channel_id=1, source_target_pairs={{0,1},{1,0},{2,3},{3,2},{4,5},{5,4},{6,7},{7,6},{8,9},{9,8},{10,11... | collective-permute-start | bytes 393224 | tf_op jit(solution)/shard_map/ppermute | solution.py:279
  61.1 10.3 %collective-permute-start.12 = (bf16[2,64,512]{2,1,0:T(8,128)(2,1)S(1)}, bf16[2,64,512]{2,1,0:T(8,128)(2,1)S(1)}, u32[]{:S(2)}, u32[]{:S(2)}) collective-permute-start(bf16[2,64,512]{2,1,0:T(8,128)(2,1)S(1)} %collective-permute-done.11.refs_12_), channel_id=1, source_target_pairs={{0,1},{1,0},{2,3},{3,2},{4,5},{5,4},{6,7},{7,6},{8,9},{9,8},{10,11... | collective-permute-start | bytes 393224 | tf_op jit(solution)/shard_map/ppermute | solution.py:279
  61.5 9.9 %collective-permute-start.14 = (bf16[2,64,512]{2,1,0:T(8,128)(2,1)S(1)}, bf16[2,64,512]{2,1,0:T(8,128)(2,1)S(1)}, u32[]{:S(2)}, u32[]{:S(2)}) collective-permute-start(bf16[2,64,512]{2,1,0:T(8,128)(2,1)S(1)} %collective-permute-done.13.refs_14_), channel_id=1, source_target_pairs={{0,1},{1,0},{2,3},{3,2},{4,5},{5,4},{6,7},{7,6},{8,9},{9,8},{10,11... | collective-permute-start | bytes 393224 | tf_op jit(solution)/shard_map/ppermute | solution.py:279
  65.7 11.8 %collective-permute-start.33 = (bf16[2,128,512]{2,1,0:T(8,128)(2,1)S(1)}, bf16[2,128,512]{2,1,0:T(8,128)(2,1)S(1)}, u32[]{:S(2)}, u32[]{:S(2)}) collective-permute-start(bf16[2,128,512]{2,1,0:T(8,128)(2,1)S(1)} %get-tuple-element.56), channel_id=1, source_target_pairs={{0,2},{1,3},{2,0},{3,1},{4,6},{5,7},{6,4},{7,5},{8,10},{9,11},{10,... | collective-permute-start | bytes 786440 | tf_op jit(solution)/shard_map/ppermute | solution.py:271
  66.5 12.0 %collective-permute-start.34 = (bf16[2,128,512]{2,1,0:T(8,128)(2,1)S(1)}, bf16[2,128,512]{2,1,0:T(8,128)(2,1)S(1)}, u32[]{:S(2)}, u32[]{:S(2)}) collective-permute-start(bf16[2,128,512]{2,1,0:T(8,128)(2,1)S(1)} %get-tuple-element.57), channel_id=1, source_target_pairs={{0,4},{1,5},{2,6},{3,7},{4,0},{5,1},{6,2},{7,3},{8,12},{9,13},{10,... | collective-permute-start | bytes 786440 | tf_op jit(solution)/shard_map/ppermute | solution.py:271
  70.7 13.4 %collective-permute-start.35 = (bf16[2,128,512]{2,1,0:T(8,128)(2,1)S(1)}, bf16[2,128,512]{2,1,0:T(8,128)(2,1)S(1)}, u32[]{:S(2)}, u32[]{:S(2)}) collective-permute-start(bf16[2,128,512]{2,1,0:T(8,128)(2,1)S(1)} %get-tuple-element.58), channel_id=1, source_target_pairs={{0,6},{1,7},{2,4},{3,5},{4,2},{5,3},{6,0},{7,1},{8,14},{9,15},{10,... | collective-permute-start | bytes 786440 | tf_op jit(solution)/shard_map/ppermute | solution.py:271
  74.5 16.7 %collective-permute-start.15 = (bf16[2,128,512]{2,1,0:T(8,128)(2,1)S(1)}, bf16[2,128,512]{2,1,0:T(8,128)(2,1)S(1)}, u32[]{:S(2)}, u32[]{:S(2)}) collective-permute-start(bf16[2,128,512]{2,1,0:T(8,128)(2,1)S(1)} %get-tuple-element.44), channel_id=1, source_target_pairs={{0,2},{1,3},{2,0},{3,1},{4,6},{5,7},{6,4},{7,5},{8,10},{9,11},{10,... | collective-permute-start | bytes 786440 | tf_op jit(solution)/shard_map/ppermute | solution.py:271
  75.5 15.7 %collective-permute-start.16 = (bf16[2,128,512]{2,1,0:T(8,128)(2,1)S(1)}, bf16[2,128,512]{2,1,0:T(8,128)(2,1)S(1)}, u32[]{:S(2)}, u32[]{:S(2)}) collective-permute-start(bf16[2,128,512]{2,1,0:T(8,128)(2,1)S(1)} %get-tuple-element.45), channel_id=1, source_target_pairs={{0,4},{1,5},{2,6},{3,7},{4,0},{5,1},{6,2},{7,3},{8,12},{9,13},{10,... | collective-permute-start | bytes 786440 | tf_op jit(solution)/shard_map/ppermute | solution.py:271
  77.4 16.9 %collective-permute-start.17 = (bf16[2,128,512]{2,1,0:T(8,128)(2,1)S(1)}, bf16[2,128,512]{2,1,0:T(8,128)(2,1)S(1)}, u32[]{:S(2)}, u32[]{:S(2)}) collective-permute-start(bf16[2,128,512]{2,1,0:T(8,128)(2,1)S(1)} %get-tuple-element.46), channel_id=1, source_target_pairs={{0,6},{1,7},{2,4},{3,5},{4,2},{5,3},{6,0},{7,1},{8,14},{9,15},{10,... | collective-permute-start | bytes 786440 | tf_op jit(solution)/shard_map/ppermute | solution.py:271
  101.6 5.0 %collective-permute-start.37 = (bf16[16,2048]{1,0:T(8,128)(2,1)S(1)}, bf16[16,2048]{1,0:T(8,128)(2,1)S(1)}, u32[]{:S(2)}, u32[]{:S(2)}) collective-permute-start(bf16[16,2048]{1,0:T(8,128)(2,1)S(1)} %get-tuple-element.63), channel_id=1, source_target_pairs={{0,1},{1,2},{2,3},{3,4},{4,5},{5,6},{6,7},{7,0},{8,9},{9,10},{10,1... | collective-permute-start | bytes 196616 | tf_op jit(solution)/shard_map/ppermute | solution.py:323
  101.7 18.5 %collective-permute-start.36 = (bf16[64,2048]{1,0:T(8,128)(2,1)S(1)}, bf16[64,2048]{1,0:T(8,128)(2,1)S(1)}, u32[]{:S(2)}, u32[]{:S(2)}) collective-permute-start(bf16[64,2048]{1,0:T(8,128)(2,1)S(1)} %get-tuple-element.62), channel_id=1, source_target_pairs={{0,8},{1,9},{2,10},{3,11},{4,12},{5,13},{6,14},{7,15},{8,0},{9,1},... | collective-permute-start | bytes 786440 | tf_op jit(solution)/shard_map/ppermute | solution.py:319
  104.4 7.5 %collective-permute-start.38 = (bf16[16,2048]{1,0:T(8,128)(2,1)S(1)}, bf16[16,2048]{1,0:T(8,128)(2,1)S(1)}, u32[]{:S(2)}, u32[]{:S(2)}) collective-permute-start(bf16[16,2048]{1,0:T(8,128)(2,1)S(1)} %get-tuple-element.64), channel_id=1, source_target_pairs={{1,0},{2,1},{3,2},{4,3},{5,4},{6,5},{7,6},{0,7},{9,8},{10,9},{11,1... | collective-permute-start | bytes 196616 | tf_op jit(solution)/shard_map/ppermute | solution.py:324
  112.0 8.2 %collective-permute-start.39 = (bf16[16,2048]{1,0:T(8,128)(2,1)S(1)}, bf16[16,2048]{1,0:T(8,128)(2,1)S(1)}, u32[]{:S(2)}, u32[]{:S(2)}) collective-permute-start(bf16[16,2048]{1,0:T(8,128)(2,1)S(1)} %get-tuple-element.73), channel_id=1, source_target_pairs={{0,8},{1,9},{2,10},{3,11},{4,12},{5,13},{6,14},{7,15},{8,0},{9,1},... | collective-permute-start | bytes 196616 | tf_op jit(solution)/shard_map/ppermute | solution.py:329
  (23 other events, 183.5 us)

commit v3 on v2

v3 whole, which is shorter than its diff:
```python
import functools
import math

import jax
import jax.numpy as jnp
import numpy as np
from jax import lax
from jax.experimental import pallas as pl
from jax.experimental.pallas import tpu as pltpu
from jax.sharding import PartitionSpec as P

DMAX = 8
LANES = 128
BF16 = jnp.bfloat16
F32 = jnp.float32
DEVICE, CHIP, MEMBER, CORE, SEG, FIRST, LAST = range(7)
SMEM = pl.BlockSpec(memory_space=pltpu.SMEM)
VMEM = pl.BlockSpec(memory_space=pltpu.VMEM)
ANY = pl.BlockSpec(memory_space=pl.ANY)


def params(mebibytes):
    return pltpu.CompilerParams(vmem_limit_bytes=mebibytes * 1024 * 1024)


def cost(flops, moved):
    return pl.CostEstimate(flops=flops, bytes_accessed=moved, transcendentals=0)


def dft_table(rows, cols, length):
    products = rows[:, None].astype(np.int64) * cols[None, :] % length
    angle = products.astype(np.float32) * np.float32(2.0 * math.pi / length)
    return np.cos(angle), -np.sin(angle)


def dot(x, y):
    return jnp.dot(x, y, preferred_element_type=F32)


def run_copies(copies):
    for copy in copies:
        copy.start()
    for copy in copies:
        copy.wait()


def piece_of(x_ref, place_ref, turn, comps, groups):
    cols = x_ref.shape[-1] // groups
    chip = place_ref[CHIP] ^ turn
    begin = pl.multiple_of(chip % groups * cols, cols)
    return x_ref.at[chip // groups, pl.ds(comps[0], comps[1]), :, pl.ds(begin, cols)]


def pack_kernel(cuts, groups, place_ref, x_ref, *refs):
    out_refs, sem = refs[:-1], refs[-1]
    run_copies(
        [
            pltpu.make_async_copy(piece_of(x_ref, place_ref, turn, comps, groups), out_ref, sem.at[at])
            for at, ((turn, comps), out_ref) in enumerate(zip(cuts, out_refs))
        ]
    )


def pack(series, place, cuts, groups):
    _, _, rows, width = series.shape
    shapes = [(comps[1], rows, width // groups) for _, comps in cuts]
    return pl.pallas_call(
        functools.partial(pack_kernel, cuts, groups),
        in_specs=[SMEM, ANY],
        out_specs=[ANY] * len(cuts),
        out_shape=[jax.ShapeDtypeStruct(shape, BF16) for shape in shapes],
        scratch_shapes=[pltpu.SemaphoreType.DMA((len(cuts),))],
        compiler_params=params(2),
        cost_estimate=cost(0, 4 * sum(math.prod(shape) for shape in shapes)),
        name="pack",
    )(place, series)


def join_kernel(turns, chips, groups, place_ref, x_ref, *refs):
    piece_refs, out_ref, sem = refs[: len(turns)], refs[-2], refs[-1]
    far = chips - groups
    moves = []
    for turn, piece_ref in zip(turns, piece_refs):
        if turn >= groups:
            moves.append((piece_ref, turn - groups))
        else:
            moves += [(piece_ref.at[pl.ds(2 * k, 2)], far + k * groups + turn) for k in range(2)]
    if out_ref.shape[0] > far:
        moves += [(piece_of(x_ref, place_ref, 0, (2 * k, 2), groups), far + k * groups) for k in range(2)]
    run_copies(
        [
            pltpu.make_async_copy(source, out_ref.at[slot], sem.at[at])
            for at, (source, slot) in enumerate(moves)
        ]
    )


def join(series, place, pieces, turns, slots, chips, groups, after):
    shape = (slots, 2) + pieces[0].shape[1:]
    return pl.pallas_call(
        functools.partial(join_kernel, turns, chips, groups),
        in_specs=[SMEM] + [ANY] * (1 + len(pieces) + len(after)),
        out_specs=ANY,
        out_shape=jax.ShapeDtypeStruct(shape, BF16),
        scratch_shapes=[pltpu.SemaphoreType.DMA((slots,))],
        compiler_params=params(2),
        cost_estimate=cost(0, 4 * math.prod(shape)),
        name="join",
    )(place, series, *pieces, *after)


def first_kernel(near_slot, groups, place_ref, *refs):
    near_refs, far_refs, refs = refs[:2], refs[2:4], refs[4:]
    w_refs, t_refs, turn_refs = refs[:2], refs[2:4], refs[4:6]
    out_refs, x_ref = refs[6:-1], refs[-1]
    rows = near_refs[0].shape[2]
    device = place_ref[DEVICE]
    for core in range(2):
        for turn in range(x_ref.shape[1] // rows // 2):
            begin = pl.multiple_of((device ^ (2 * turn + core)) * rows, rows)
            source = far_refs[core].at[turn - groups] if turn >= groups else near_refs[core].at[near_slot + turn]
            x_ref[:, pl.ds(begin, rows), :] = source[...]

    height = out_refs[0].shape[1]
    cols = x_ref.shape[-1]
    tile = min(256, cols)
    owners = [place_ref[CORE] * groups + (place_ref[MEMBER] ^ turn) for turn in range(groups)]
    spots = [pl.ds(pl.multiple_of(owner * height, height), height) for owner in owners]
    stack = lambda ref: jnp.concatenate([ref[spot, :] for spot in spots], axis=0)
    for begin in range(0, cols, tile):
        at = slice(begin, begin + tile)
        x_real, x_imag = x_ref[0, :, at], x_ref[1, :, at]
        w_real, w_imag = stack(w_refs[0]), stack(w_refs[1])
        real_part = dot(w_real, x_real) - dot(w_imag, x_imag)
        imag_part = dot(w_imag, x_real) + dot(w_real, x_imag)
        for turn, (out_ref, spot) in enumerate(zip(out_refs, spots)):
            part = slice(turn * height, (turn + 1) * height)
            by_real, by_imag = turn_refs[0][spot, :], turn_refs[1][spot, :]
            base_real, base_imag = t_refs[0][spot, at], t_refs[1][spot, at]
            t_real = base_real * by_real - base_imag * by_imag
            t_imag = base_real * by_imag + base_imag * by_real
            out_ref[0, :, at] = (real_part[part] * t_real - imag_part[part] * t_imag).astype(BF16)
            out_ref[1, :, at] = (real_part[part] * t_imag + imag_part[part] * t_real).astype(BF16)


def first_pass(near_slot, near, far, place, tables, twiddles, turns, groups):
    _, _, rows, cols = near[0].shape
    length = tables[0].shape[0]
    height = length // 2 // groups
    return pl.pallas_call(
        functools.partial(first_kernel, near_slot, groups),
        in_specs=[SMEM] + [VMEM] * 10,
        out_specs=[VMEM] * groups,
        out_shape=[jax.ShapeDtypeStruct((2, height, cols), BF16)] * groups,
        scratch_shapes=[pltpu.VMEM((2, length, cols), BF16)],
        compiler_params=params(16),
        cost_estimate=cost(4 * length * length * cols, 4 * length * length),
        name="first_pass",
    )(place, *near, *far, *tables, *twiddles, *turns)


def gather_rows(place_ref, piece_refs, lhs_ref):
    cols = piece_refs[0].shape[-1]
    height = lhs_ref.shape[0] // 2
    odd = lax.broadcasted_iota(jnp.int32, (height, cols), 1) % 2 == 1
    for turn, piece_ref in enumerate(piece_refs):
        at = pl.ds(pl.multiple_of((place_ref[MEMBER] ^ turn) * cols, cols), cols)
        piece = piece_ref[...].reshape(height, cols)
        lhs_ref[:height, at] = piece
        lhs_ref[height:, at] = jnp.where(odd, -piece, piece)


def transform(lhs_ref, w_refs, at, store):
    by_real = dot(lhs_ref[...], w_refs[0][:, at])
    by_imag = dot(lhs_ref[...], w_refs[1][:, at])
    rows = lhs_ref.shape[0] // 4
    for half in range(2):
        upper = slice(2 * half * rows, (2 * half + 1) * rows)
        lower = slice((2 * half + 1) * rows, (2 * half + 2) * rows)
        store(half, by_real[upper] - by_imag[lower], by_imag[upper] + by_real[lower])


def second_kernel(groups, place_ref, *refs):
    w_refs, (re_ref, im_ref, lhs_ref) = refs[groups : groups + 2], refs[groups + 2 :]
    gather_rows(place_ref, refs[:groups], lhs_ref)
    span = w_refs[0].shape[1]
    tile = min(256, span)

    def store(begin, half, real_part, imag_part):
        at = pl.ds(pl.multiple_of(half * span + begin, tile), tile)
        re_ref[:, at] = real_part
        im_ref[:, at] = imag_part

    @pl.loop(0, span // tile)
    def _(step):
        begin = pl.multiple_of(step * tile, tile)
        transform(lhs_ref, w_refs, pl.ds(begin, tile), functools.partial(store, begin))


def fstat_kernel(groups, place_ref, coef_ref, *refs):
    w_refs, refs, piece_refs = refs[groups : groups + 2], refs[groups + 2 :], refs[:groups]
    ar_ref, ai_ref, other_ref, own_ref, tail_refs, head_refs, lhs_ref = *refs[:4], refs[4:6], refs[6:8], refs[8]
    gather_rows(place_ref, piece_refs, lhs_ref)
    span = w_refs[0].shape[1]
    tile = min(256, span)
    rows = own_ref.shape[0]
    is_first = place_ref[SEG] == 0
    last_member = 2 * groups - 1
    member = 2 * place_ref[MEMBER] + place_ref[CORE]
    tail_first = jnp.where(member == last_member, 1 - place_ref[SEG], place_ref[SEG]) == 0
    head_first = jnp.where(member == 0, 1 - place_ref[SEG], place_ref[SEG]) == 0

    def store(begin, half, b_real, b_imag):
        at = pl.ds(pl.multiple_of(half * span + begin, tile), tile)
        a_real, a_imag = ar_ref[:, at], ai_ref[:, at]
        fstat = (
            coef_ref[1] * (a_real * a_real + a_imag * a_imag)
            + coef_ref[0] * (b_real * b_real + b_imag * b_imag)
            - coef_ref[2] * (a_real * b_real + a_imag * b_imag)
        )
        first, last = fstat[:rows], fstat[rows:]
        own_ref[:, at] = jnp.where(is_first, first, last)
        other_ref[:, at] = jnp.where(is_first, last, first).astype(BF16)
        rims = pl.ds(half * DMAX, DMAX), pl.ds(begin, tile)
        tails, heads = (first[rows - DMAX :], last[rows - DMAX :]), (first[:DMAX], last[:DMAX])
        for refs, pair, takes_first in ((tail_refs, tails, tail_first), (head_refs, heads, head_first)):
            refs[0][rims] = jnp.where(takes_first, pair[0], pair[1])
            refs[1][rims] = jnp.where(takes_first, pair[1], pair[0])

    @pl.loop(0, span // tile)
    def _(step):
        begin = pl.multiple_of(step * tile, tile)
        transform(lhs_ref, w_refs, pl.ds(begin, tile), functools.partial(store, begin))


def second_pass(pieces, place, tables):
    groups = len(pieces)
    _, height, cols = pieces[0].shape
    width = groups * cols
    return pl.pallas_call(
        functools.partial(second_kernel, groups),
        in_specs=[SMEM] + [VMEM] * (groups + 2),
        out_specs=[VMEM] * 2,
        out_shape=[jax.ShapeDtypeStruct((height, width), F32)] * 2,
        scratch_shapes=[pltpu.VMEM((4 * height, width), BF16)],
        compiler_params=params(16),
        cost_estimate=cost(8 * height * width * width, 2 * width * width),
        name="second_pass",
    )(place, *pieces, *tables)


def fstat_pass(pieces, place, tables, spectrum, coefs, rows):
    groups = len(pieces)
    _, height, cols = pieces[0].shape
    width = groups * cols
    rim = jax.ShapeDtypeStruct((2 * DMAX, width // 2), F32)
    return pl.pallas_call(
        functools.partial(fstat_kernel, groups),
        in_specs=[SMEM, SMEM] + [VMEM] * (groups + 4),
        out_specs=[VMEM] * 6,
        out_shape=[
            jax.ShapeDtypeStruct((rows, width), BF16),
            jax.ShapeDtypeStruct((rows, width), F32),
        ]
        + [rim] * 4,
        scratch_shapes=[pltpu.VMEM((4 * height, width), BF16)],
        compiler_params=params(16),
        cost_estimate=cost(8 * height * width * width, 2 * width * width),
        name="fstat_pass",
    )(place, coefs, *pieces, *tables, *spectrum)


def detect_kernel(offsets_ref, place_ref, other_ref, own_ref, *refs):
    rim_refs, out_ref, wide_refs = refs[:4], refs[4], refs[5:]
    rows = own_ref.shape[0]

    @pl.when(pl.program_id(0) == 0)
    def _():
        is_first, is_last, seg = place_ref[FIRST] == 1, place_ref[LAST] == 1, place_ref[SEG]
        width = own_ref.shape[1]

        def widen(wide_ref, middle, lower_ref, upper_ref):
            lower = jnp.concatenate([lower_ref[:DMAX], lower_ref[DMAX:]], axis=1)
            upper = jnp.concatenate([upper_ref[:DMAX], upper_ref[DMAX:]], axis=1)
            lower = jnp.where(is_first, pltpu.roll(lower, 1, 1), lower)
            upper = jnp.where(is_last, pltpu.roll(upper, width - 1, 1), upper)
            for strip in range(width // LANES):
                at = slice(strip * LANES, (strip + 1) * LANES)
                wide_ref[strip, :DMAX] = lower[:, at]
                wide_ref[strip, DMAX : DMAX + rows] = middle[:, at]
                wide_ref[strip, DMAX + rows :] = upper[:, at]

        def place(own_wide, other_wide):
            widen(own_wide, own_ref[...], *rim_refs[:2])
            widen(other_wide, other_ref[...].astype(F32), *rim_refs[2:])

        @pl.when(seg == 0)
        def _():
            place(wide_refs[0], wide_refs[1])

        @pl.when(seg != 0)
        def _():
            place(wide_refs[1], wide_refs[0])

    template = pl.program_id(0)
    begins = [DMAX + offsets_ref[template, s] for s in range(len(wide_refs))]
    for strip in range(own_ref.shape[1] // LANES):
        total = wide_refs[0][strip, pl.ds(begins[0], rows), :]
        for begin, wide_ref in zip(begins[1:], wide_refs[1:]):
            total = total + wide_ref[strip, pl.ds(begin, rows), :]
        out_ref[0, :, strip * LANES : (strip + 1) * LANES] = total * (1.0 / len(wide_refs))


def detect(offsets, place, other, own, rims):
    templates = offsets.shape[0]
    rows, width = own.shape
    return pl.pallas_call(
        detect_kernel,
        grid=(templates,),
        in_specs=[SMEM, SMEM] + [VMEM] * 6,
        out_specs=pl.BlockSpec((1, rows, width), lambda t: (t, 0, 0)),
        out_shape=jax.ShapeDtypeStruct((templates, rows, width), F32),
        scratch_shapes=[pltpu.VMEM((width // LANES, rows + 2 * DMAX, LANES), F32)] * 2,
        compiler_params=params(8),
        cost_estimate=cost(3 * templates * rows * width, 4 * templates * rows * width),
        name="detect",
    )(offsets, place, other, own, *rims)


def local(series, antenna, offsets):
    devices = lax.axis_size("tm")
    index = lax.axis_index("tm")
    segs, _, rows, width = series.shape
    slow = devices * rows
    length = slow * width
    chips = devices // 2
    groups = chips // segs
    cols = width // groups
    core, chip = index % 2, index // 2
    seg, member = chip // groups, chip % groups
    place = jnp.stack([index, chip, member, core, seg, index == 0, index == devices - 1]).astype(jnp.int32)

    bins = np.arange(slow).reshape(segs, groups, 2, rows).transpose(2, 1, 0, 3).reshape(-1)
    short = [x.astype(BF16) for x in dft_table(bins, np.arange(slow), slow)]
    long = [x.astype(BF16) for x in dft_table(np.arange(width), np.arange(width // 2), width)]
    twiddles = dft_table(bins, np.arange(cols), length)
    angle = (jnp.asarray(bins, jnp.int32) * (member * cols) % length).astype(F32) * (2.0 * math.pi / length)
    turns = (jnp.cos(angle)[:, None], -jnp.sin(angle)[:, None])

    def send(piece, turn):
        return lax.ppermute(piece, "tm", [(i, i ^ turn) for i in range(devices)])

    def pass_on(pieces):
        return [pieces[0]] + [send(x, 2 * turn) for turn, x in enumerate(pieces) if turn]

    far_turns = list(range(groups, chips))[::-1]
    near_turns = list(range(1, groups))[::-1]
    half = len(far_turns) // 2
    both, series_a, series_b = (0, 4), (0, 2), (2, 2)
    cuts_a = [(turn, series_a) for turn in far_turns]
    cuts_a = cuts_a[:half] + [(turn, both) for turn in near_turns] + cuts_a[half:]
    cuts_b = [(turn, series_b) for turn in far_turns]
    packed = pack(series, place, cuts_a + cuts_b, groups)
    turns_a, turns_b = [turn for turn, _ in cuts_a], [turn for turn, _ in cuts_b]
    sent = [send(x, 2 * turn) for x, turn in zip(packed, turns_a + turns_b)]
    sent_a, sent_b = sent[: len(cuts_a)], sent[len(cuts_a) :]

    def pass_one(series_at, near, joined):
        slot = chips - groups + series_at * groups
        return pass_on(first_pass(slot, near, joined, place, short, twiddles, turns, groups))

    joined = join(series, place, sent_a, turns_a, chips + groups, chips, groups, sent_b[:1])
    near = (joined, send(joined, 1))
    turned = [pass_one(0, near, near)]
    joined = join(series, place, sent_b, turns_b, chips - groups, chips, groups, turned[0][1:2])
    turned.append(pass_one(1, near, (joined, send(joined, 1))))
    spectrum = second_pass(turned[0], place, long)
    coef = lax.dynamic_index_in_dim(antenna, seg, 0, keepdims=False)
    scale = (coef[0] * coef[1] - coef[2] * coef[2]) * length
    coefs = coef * jnp.array([1.0, 1.0, 2.0], F32) / scale
    other, own, tail, far_tail, head, far_head = fstat_pass(turned[1], place, long, spectrum, coefs, rows)

    members = 2 * groups
    def moved(x, across, by):
        half_of = lambda i: (i // members + across) % segs * members
        return lax.ppermute(x, "tm", [(i, half_of(i) + (i + by) % members) for i in range(devices)])

    other = moved(other, 1, 0)
    rims = [moved(tail, 0, 1), moved(head, 0, -1), moved(far_tail, 1, 1), moved(far_head, 1, -1)]
    return detect(offsets, place, other, own, rims)


def solution(mesh):
    return jax.shard_map(
        local,
        mesh=mesh,
        in_specs=(P("sky", None, "tm", None), P("sky", None), P("sky", None)),
        out_specs=P("sky", "tm", None),
        check_vma=False,
    )
```

time: 125 us -> 140 us (1.12)
  local copies, waits for them, and re-layouts: 8.13 us -> 21.4 us
  other arithmetic: 4.51 us -> 0.06 us
  starting transfers between devices: 43 us -> 45.7 us
  between operations: 0.34 us -> 2.83 us
    unnamed x31 -> x61, local copies, waits for them, and re-layouts: 6.22 us -> 18.6 us
    neg x1, other arithmetic: 4.19 us -> 0.05 us  [local(): turns = (jnp.cos(angle)[:, None], -jnp.sin(angle)[:, None])]
    ppermute x40 -> x24, starting transfers between devices: 43 us -> 45.7 us  [the longest x19 37.4 us: send(): return lax.ppermute(piece, 'tm', [(i, i ^ turn) for i in range(devices)])]
    another operation x3 -> x1, local copies, waits for them, and re-layouts: 1.82 us -> 0.08 us  [local(): jnp.stack([index, chip, member, core, seg, index == 0, index == devices -...]
    ppermute x40 -> x24, waiting for transfers between devices: 40.2 us -> 41.2 us  [the longest x19 30.6 us: send(): return lax.ppermute(piece, 'tm', [(i, i ^ turn) for i in range(devices)])]
    pallas_call x6 -> x7, Pallas kernels: 24.1 us -> 23.9 us  [the longest x2 7.38 us: first_pass(): pl.pallas_call(functools.partial(first_kernel, near_slot, groups), in_spe...]
  transfers between devices with their start and end apart: 40 -> 24, of which waited for: 8 -> 12; matrix products, arithmetic and copies ran while one was open for 5% -> 2% of each run, Pallas kernels for 12% -> 7%
where the time goes in v3:
time: 140 us
  starting transfers between devices  45.7 us (33%)
  waiting for transfers between devices  41.2 us (29%)
  Pallas kernels  28.4 us (20%)
  local copies, waits for them, and re-layouts  21.4 us (15%)
  between operations  2.83 us (2%)
    ppermute x19, starting transfers between devices, send(): return lax.ppermute(piece, 'tm', [(i, i ^ turn) for i in range(devices)])  37.4 us
    ppermute x19, waiting for transfers between devices, send(): return lax.ppermute(piece, 'tm', [(i, i ^ turn) for i in range(devices)])  30.6 us
    unnamed x61, local copies, waits for them, and re-layouts  18.6 us
    ppermute x5, waiting for transfers between devices, moved(): lax.ppermute(x, 'tm', [(i, half_of(i) + (i + by) % members) for i in rang...  10.6 us
    ppermute x5, starting transfers between devices, moved(): lax.ppermute(x, 'tm', [(i, half_of(i) + (i + by) % members) for i in rang...  8.28 us
    pallas_call x2, Pallas kernels, first_pass(): pl.pallas_call(functools.partial(first_kernel, near_slot, groups), in_spe...  7.38 us
    pallas_call x1, Pallas kernels, fstat_pass(): pl.pallas_call(functools.partial(fstat_kernel, groups), in_specs=[SMEM, S...  6.01 us
    pallas_call x1, Pallas kernels, second_pass(): pl.pallas_call(functools.partial(second_kernel, groups), in_specs=[SMEM]...  5.84 us
  transfers between devices with their start and end apart: 24, of which 12 were waited for; matrix products, arithmetic and copies ran while one was open for 2% of the time, Pallas kernels for 7%

profile of v3, /device:TPU:0, one launch (start us, length us, event | category | flops | bytes accessed | tf_op | source)
XLA Modules:
  0.0 139.7 jit_solution(11278004737436107203)
XLA Ops:
  0.1 1.6 %copy-done = bf16[2,4,64,2048]{3,2,1,0:T(8,128)(2,1)S(1)} copy-done((bf16[2,4,64,2048]{3,2,1,0:T(8,128)(2,1)S(1)}, bf16[2,4,64,2048]{3,2,1,0:T(8,128)(2,1)}, u32[]{:S(2)}) %copy-start) | copy-done | bytes 2097176
  2.6 6.1 %collective-permute-start = (bf16[2,64,512]{2,1,0:T(8,128)(2,1)S(1)}, bf16[2,64,512]{2,1,0:T(8,128)(2,1)S(1)}, u32[]{:S(2)}, u32[]{:S(2)}) collective-permute-start(bf16[2,64,512]{2,1,0:T(8,128)(2,1)S(1)} %get-tuple-element.32), channel_id=1, source_target_pairs={{0,14},{1,15},{2,12},{3,13},{4,10},{5,11},{6,8},{7,9},{8,6},{9,7},... | collective-permute-start | bytes 393224 | tf_op jit(solution)/shard_map/ppermute | solution.py:351
  9.7 4.3 %collective-permute-start.2 = (bf16[4,64,512]{2,1,0:T(8,128)(2,1)S(1)}, bf16[4,64,512]{2,1,0:T(8,128)(2,1)S(1)}, u32[]{:S(2)}, u32[]{:S(2)}) collective-permute-start(bf16[4,64,512]{2,1,0:T(8,128)(2,1)S(1)} %get-tuple-element.34), channel_id=1, source_target_pairs={{0,6},{1,7},{2,4},{3,5},{4,2},{5,3},{6,0},{7,1},{8,14},{9,15},{10,... | collective-permute-start | bytes 786440 | tf_op jit(solution)/shard_map/ppermute | solution.py:351
  14.6 2.4 %collective-permute-done.1.refs_1_ = bf16[2,64,512]{2,1,0:T(8,128)(2,1)S(1)} collective-permute-done((bf16[2,64,512]{2,1,0:T(8,128)(2,1)S(1)}, bf16[2,64,512]{2,1,0:T(8,128)(2,1)S(1)}, u32[]{:S(2)}, u32[]{:S(2)}) %collective-permute-start.1) | collective-permute-done | bytes 131104 | tf_op jit(solution)/shard_map/ppermute | solution.py:351
  16.9 8.8 %collective-permute-start.6 = (bf16[2,64,512]{2,1,0:T(8,128)(2,1)S(1)}, bf16[2,64,512]{2,1,0:T(8,128)(2,1)S(1)}, u32[]{:S(2)}, u32[]{:S(2)}) collective-permute-start(bf16[2,64,512]{2,1,0:T(8,128)(2,1)S(1)} %get-tuple-element.38), channel_id=1, source_target_pairs={{0,8},{1,9},{2,10},{3,11},{4,12},{5,13},{6,14},{7,15},{8,0},{9,1},... | collective-permute-start | bytes 393224 | tf_op jit(solution)/shard_map/ppermute | solution.py:351
  26.4 4.1 %collective-permute-start.7 = (bf16[2,64,512]{2,1,0:T(8,128)(2,1)S(1)}, bf16[2,64,512]{2,1,0:T(8,128)(2,1)S(1)}, u32[]{:S(2)}, u32[]{:S(2)}) collective-permute-start(bf16[2,64,512]{2,1,0:T(8,128)(2,1)S(1)} %get-tuple-element.39), channel_id=1, source_target_pairs={{0,14},{1,15},{2,12},{3,13},{4,10},{5,11},{6,8},{7,9},{8,6},{9,7},... | collective-permute-start | bytes 393224 | tf_op jit(solution)/shard_map/ppermute | solution.py:351
  30.5 2.6 %collective-permute-done.6.refs_6_ = bf16[2,64,512]{2,1,0:T(8,128)(2,1)S(1)} collective-permute-done((bf16[2,64,512]{2,1,0:T(8,128)(2,1)S(1)}, bf16[2,64,512]{2,1,0:T(8,128)(2,1)S(1)}, u32[]{:S(2)}, u32[]{:S(2)}) %collective-permute-start.6) | collective-permute-done | bytes 131104 | tf_op jit(solution)/shard_map/ppermute | solution.py:351
  33.1 4.1 %collective-permute-done.7.refs_7_.refs_0_ = bf16[2,64,512]{2,1,0:T(8,128)(2,1)S(1)} collective-permute-done((bf16[2,64,512]{2,1,0:T(8,128)(2,1)S(1)}, bf16[2,64,512]{2,1,0:T(8,128)(2,1)S(1)}, u32[]{:S(2)}, u32[]{:S(2)}) %collective-permute-start.7) | collective-permute-done | bytes 131104 | tf_op jit(solution)/shard_map/ppermute | solution.py:351
  37.2 2.4 %join.2.refs_0_.refs_2_ = bf16[12,2,64,512]{3,2,1,0:T(8,128)(2,1)S(1)} custom-call(s32[7]{0:T(128)S(1)} %stack.39.place_ref, bf16[2,4,64,2048]{3,2,1,0:T(8,128)(2,1)S(1)} %copy-done, bf16[2,64,512]{2,1,0:T(8,128)(2,1)S(1)} %collective-permute-done.refs_0_, bf16[2,64,512]{2,1,0:T(8,128)(2,1)S(1)} %collective-permute-done.1.refs_1_, ...), custom_call_target="tpu_custom_call" | custom-call | bytes 3145728 | tf_op jit(solution)/shard_map/join/pallas_call | solution.py:100
  43.1 1.6 %copy-done.2 = f32[1024,512]{1,0:T(8,128)S(1)} copy-done((f32[1024,512]{1,0:T(8,128)S(1)}, f32[1024,512]{1,0:T(8,128)}, u32[]{:S(2)}) %copy-start.2) | copy-done | bytes 2097176
  44.7 1.6 %copy-done.4 = f32[1024,512]{1,0:T(8,128)S(1)} copy-done((f32[1024,512]{1,0:T(8,128)S(1)}, f32[1024,512]{1,0:T(8,128)}, u32[]{:S(2)}) %copy-start.4) | copy-done | bytes 2097176
  46.3 1.6 %copy-done.6 = bf16[1024,1024]{1,0:T(8,128)(2,1)S(1)} copy-done((bf16[1024,1024]{1,0:T(8,128)(2,1)S(1)}, bf16[1024,1024]{1,0:T(8,128)(2,1)}, u32[]{:S(2)}) %copy-start.6) | copy-done | bytes 2097176
  47.9 1.6 %copy-done.8 = bf16[1024,1024]{1,0:T(8,128)(2,1)S(1)} copy-done((bf16[1024,1024]{1,0:T(8,128)(2,1)S(1)}, bf16[1024,1024]{1,0:T(8,128)(2,1)}, u32[]{:S(2)}) %copy-start.8) | copy-done | bytes 2097176
  51.6 3.3 %first_pass.2 = (bf16[2,128,512]{2,1,0:T(8,128)(2,1)S(1)}, bf16[2,128,512]{2,1,0:T(8,128)(2,1)S(1)}, bf16[2,128,512]{2,1,0:T(8,128)(2,1)S(1)}, bf16[2,128,512]{2,1,0:T(8,128)(2,1)S(1)}) custom-call(s32[7]{0:T(128)S(1)} %stack.39.place_ref, bf16[12,2,64,512]{3,2,1,0:T(8,128)(2,1)S(1)} %join.2.refs_0_.refs_2_, ...), custom_call_target="tpu_custom_call" | custom-call | flops 2147483648 | bytes 4194304 | tf_op jit(solution)/shard_map/first_pass/pallas_call | solution.py:150
  56.4 2.0 %collective-permute-start.9 = (bf16[2,64,512]{2,1,0:T(8,128)(2,1)S(1)}, bf16[2,64,512]{2,1,0:T(8,128)(2,1)S(1)}, u32[]{:S(2)}, u32[]{:S(2)}) collective-permute-start(bf16[2,64,512]{2,1,0:T(8,128)(2,1)S(1)} %copy-done.23), channel_id=1, source_target_pairs={{0,12},{1,13},{2,14},{3,15},{4,8},{5,9},{6,10},{7,11},{8,4},{9,5},... | collective-permute-start | bytes 393224 | tf_op jit(solution)/shard_map/ppermute | solution.py:351
  58.6 2.7 %collective-permute-start.11 = (bf16[2,64,512]{2,1,0:T(8,128)(2,1)S(1)}, bf16[2,64,512]{2,1,0:T(8,128)(2,1)S(1)}, u32[]{:S(2)}, u32[]{:S(2)}) collective-permute-start(bf16[2,64,512]{2,1,0:T(8,128)(2,1)S(1)} %copy-done.19), channel_id=1, source_target_pairs={{0,8},{1,9},{2,10},{3,11},{4,12},{5,13},{6,14},{7,15},{8,0},{9,1},... | collective-permute-start | bytes 393224 | tf_op jit(solution)/shard_map/ppermute | solution.py:351
  61.4 3.3 %collective-permute-done.9.refs_1_ = bf16[2,64,512]{2,1,0:T(8,128)(2,1)S(1)} collective-permute-done((bf16[2,64,512]{2,1,0:T(8,128)(2,1)S(1)}, bf16[2,64,512]{2,1,0:T(8,128)(2,1)S(1)}, u32[]{:S(2)}, u32[]{:S(2)}) %collective-permute-start.9) | collective-permute-done | bytes 131104 | tf_op jit(solution)/shard_map/ppermute | solution.py:351
  64.7 9.5 %collective-permute-done.10.refs_2_ = bf16[2,64,512]{2,1,0:T(8,128)(2,1)S(1)} collective-permute-done((bf16[2,64,512]{2,1,0:T(8,128)(2,1)S(1)}, bf16[2,64,512]{2,1,0:T(8,128)(2,1)S(1)}, u32[]{:S(2)}, u32[]{:S(2)}) %collective-permute-start.10) | collective-permute-done | bytes 131104 | tf_op jit(solution)/shard_map/ppermute | solution.py:351
  80.3 2.4 %collective-permute-start.18 = (bf16[2,128,512]{2,1,0:T(8,128)(2,1)}, bf16[2,128,512]{2,1,0:T(8,128)(2,1)S(1)}, u32[]{:S(2)}, u32[]{:S(2)}) collective-permute-start(bf16[2,128,512]{2,1,0:T(8,128)(2,1)} %copy-done.16), channel_id=1, source_target_pairs={{0,6},{1,7},{2,4},{3,5},{4,2},{5,3},{6,0},{7,1},{8,14},{9,15},{10,... | collective-permute-start | bytes 786440 | tf_op jit(solution)/shard_map/ppermute | solution.py:351
  84.3 1.6 %copy-done.5 = f32[1024,512]{1,0:T(8,128)S(1)} copy-done((f32[1024,512]{1,0:T(8,128)S(1)}, f32[1024,512]{1,0:T(8,128)}, u32[]{:S(2)}) %copy-start.5) | copy-done | bytes 2097176
  85.9 1.6 %copy-done.7 = bf16[1024,1024]{1,0:T(8,128)(2,1)S(1)} copy-done((bf16[1024,1024]{1,0:T(8,128)(2,1)S(1)}, bf16[1024,1024]{1,0:T(8,128)(2,1)}, u32[]{:S(2)}) %copy-start.7) | copy-done | bytes 2097176
  87.5 1.6 %copy-done.9 = bf16[1024,1024]{1,0:T(8,128)(2,1)S(1)} copy-done((bf16[1024,1024]{1,0:T(8,128)(2,1)S(1)}, bf16[1024,1024]{1,0:T(8,128)(2,1)}, u32[]{:S(2)}) %copy-start.9) | copy-done | bytes 2097176
  91.2 4.1 %first_pass.3 = (bf16[2,128,512]{2,1,0:T(8,128)(2,1)S(1)}, bf16[2,128,512]{2,1,0:T(8,128)(2,1)S(1)}, bf16[2,128,512]{2,1,0:T(8,128)(2,1)S(1)}, bf16[2,128,512]{2,1,0:T(8,128)(2,1)S(1)}) custom-call(s32[7]{0:T(128)S(1)} %stack.39.place_ref, bf16[12,2,64,512]{3,2,1,0:T(8,128)(2,1)S(1)} %join.2.refs_0_.refs_2_, ...), custom_call_target="tpu_custom_call" | custom-call | flops 2147483648 | bytes 4194304 | tf_op jit(solution)/shard_map/first_pass/pallas_call | solution.py:150
  96.5 2.3 %collective-permute-start.16 = (bf16[2,128,512]{2,1,0:T(8,128)(2,1)S(1)}, bf16[2,128,512]{2,1,0:T(8,128)(2,1)S(1)}, u32[]{:S(2)}, u32[]{:S(2)}) collective-permute-start(bf16[2,128,512]{2,1,0:T(8,128)(2,1)S(1)} %get-tuple-element.47), channel_id=1, source_target_pairs={{0,6},{1,7},{2,4},{3,5},{4,2},{5,3},{6,0},{7,1},{8,14},{9,15},{10,... | collective-permute-start | bytes 786440 | tf_op jit(solution)/shard_map/ppermute | solution.py:351
  98.8 5.8 %second_pass.1 = (f32[128,2048]{1,0:T(8,128)S(1)}, f32[128,2048]{1,0:T(8,128)S(1)}) custom-call(s32[7]{0:T(128)S(1)} %stack.39.place_ref, bf16[2,128,512]{2,1,0:T(8,128)(2,1)S(1)} %copy-done.15, bf16[2,128,512]{2,1,0:T(8,128)(2,1)S(1)} %collective-permute-done.12.refs_4_.refs_1_, bf16[2,128,512]{2,1,0:T(8,128)(2,1)S(1)} %collective-permute-done.17.refs_2_, ...), custom_call_target="tpu_custom_call" | custom-call | flops 4294967296 | bytes 8388608 | tf_op jit(solution)/shard_map/second_pass/pallas_call | solution.py:240
  105.7 4.6 %collective-permute-done.16.refs_3_ = bf16[2,128,512]{2,1,0:T(8,128)(2,1)S(1)} collective-permute-done((bf16[2,128,512]{2,1,0:T(8,128)(2,1)S(1)}, bf16[2,128,512]{2,1,0:T(8,128)(2,1)S(1)}, u32[]{:S(2)}, u32[]{:S(2)}) %collective-permute-start.16) | collective-permute-done | bytes 262176 | tf_op jit(solution)/shard_map/ppermute | solution.py:351
  110.2 6.0 %fstat_pass.1 = (bf16[64,2048]{1,0:T(8,128)(2,1)S(1)}, f32[64,2048]{1,0:T(8,128)S(1)}, f32[16,1024]{1,0:T(8,128)S(1)}, f32[16,1024]{1,0:T(8,128)S(1)}, f32[16,1024]{1,0:T(8,128)S(1)}, /*index=5*/f32[16,1024]{1,0:T(8,128)S(1)}) custom-call(s32[7]{0:T(128)S(1)} %stack.39.place_ref, f32[3]{0:T(128)S(1)} %divide_bitcast_fusion.coef_ref, ...), custom_call_target="tpu_custom_call" | custom-call | flops 4294967296 | bytes 8388608 | tf_op jit(solution)/shard_map/fstat_pass/pallas_call | solution.py:257
  117.5 2.6 %collective-permute-start.21 = (f32[16,1024]{1,0:T(8,128)S(1)}, f32[16,1024]{1,0:T(8,128)S(1)}, u32[]{:S(2)}, u32[]{:S(2)}) collective-permute-start(f32[16,1024]{1,0:T(8,128)S(1)} %get-tuple-element.56), channel_id=1, source_target_pairs={{0,7},{1,0},{2,1},{3,2},{4,3},{5,4},{6,5},{7,6},{8,15},{9,8},{10,9... | collective-permute-start | bytes 196616 | tf_op jit(solution)/shard_map/ppermute | solution.py:386
  120.1 4.4 %collective-permute-start.23 = (f32[16,1024]{1,0:T(8,128)S(1)}, f32[16,1024]{1,0:T(8,128)S(1)}, u32[]{:S(2)}, u32[]{:S(2)}) collective-permute-start(f32[16,1024]{1,0:T(8,128)S(1)} %get-tuple-element.58), channel_id=1, source_target_pairs={{0,15},{1,8},{2,9},{3,10},{4,11},{5,12},{6,13},{7,14},{8,7},{9,0},... | collective-permute-start | bytes 196616 | tf_op jit(solution)/shard_map/ppermute | solution.py:386
  124.6 2.6 %collective-permute-done.22.refs_2_ = f32[16,1024]{1,0:T(8,128)S(1)} collective-permute-done((f32[16,1024]{1,0:T(8,128)S(1)}, f32[16,1024]{1,0:T(8,128)S(1)}, u32[]{:S(2)}, u32[]{:S(2)}) %collective-permute-start.22) | collective-permute-done | bytes 65568 | tf_op jit(solution)/shard_map/ppermute | solution.py:386
  127.2 7.9 %collective-permute-done.23.refs_3_ = f32[16,1024]{1,0:T(8,128)S(1)} collective-permute-done((f32[16,1024]{1,0:T(8,128)S(1)}, f32[16,1024]{1,0:T(8,128)S(1)}, u32[]{:S(2)}, u32[]{:S(2)}) %collective-permute-start.23) | collective-permute-done | bytes 65568 | tf_op jit(solution)/shard_map/ppermute | solution.py:386
  135.2 4.5 %detect.1 = f32[8,64,2048]{2,1,0:T(8,128)} custom-call(s32[8,2]{1,0:T(8,128)S(1)} %copy.17.offsets_ref, s32[7]{0:T(128)S(1)} %stack.39.place_ref, bf16[64,2048]{1,0:T(8,128)(2,1)S(1)} %collective-permute-done.19.other_ref, f32[64,2048]{1,0:T(8,128)S(1)} %get-tuple-element.54.own_ref, f32[16,1024]{1,0:T(8,128)S(1)} %collective-permute-done.20.refs_0_, ...), custom_call_target="tpu_custom_call" | custom-call | flops 3145728 | bytes 4194304 | tf_op jit(solution)/shard_map/detect/pallas_call | solution.py:317
  (92 shorter events, 21.2 us)
Async XLA Ops:
  2.6 37.0 %copy-start.18 = (bf16[2,64,512]{2,1,0:T(8,128)(2,1)}, bf16[2,64,512]{2,1,0:T(8,128)(2,1)S(1)}, u32[]{:S(2)}) copy-start(bf16[2,64,512]{2,1,0:T(8,128)(2,1)S(1)} %get-tuple-element.42) | copy-start | bytes 393220
  2.6 37.0 %copy-start.20 = (bf16[2,64,512]{2,1,0:T(8,128)(2,1)}, bf16[2,64,512]{2,1,0:T(8,128)(2,1)S(1)}, u32[]{:S(2)}) copy-start(bf16[2,64,512]{2,1,0:T(8,128)(2,1)S(1)} %get-tuple-element.41) | copy-start | bytes 393220
  2.6 37.0 %copy-start.22 = (bf16[2,64,512]{2,1,0:T(8,128)(2,1)}, bf16[2,64,512]{2,1,0:T(8,128)(2,1)S(1)}, u32[]{:S(2)}) copy-start(bf16[2,64,512]{2,1,0:T(8,128)(2,1)S(1)} %get-tuple-element.40) | copy-start | bytes 393220
  2.6 11.4 %collective-permute-start = (bf16[2,64,512]{2,1,0:T(8,128)(2,1)S(1)}, bf16[2,64,512]{2,1,0:T(8,128)(2,1)S(1)}, u32[]{:S(2)}, u32[]{:S(2)}) collective-permute-start(bf16[2,64,512]{2,1,0:T(8,128)(2,1)S(1)} %get-tuple-element.32), channel_id=1, source_target_pairs={{0,14},{1,15},{2,12},{3,13},{4,10},{5,11},{6,8},{7,9},{8,6},{9,7},... | collective-permute-start | bytes 393224 | tf_op jit(solution)/shard_map/ppermute | solution.py:351
  8.7 8.2 %collective-permute-start.1 = (bf16[2,64,512]{2,1,0:T(8,128)(2,1)S(1)}, bf16[2,64,512]{2,1,0:T(8,128)(2,1)S(1)}, u32[]{:S(2)}, u32[]{:S(2)}) collective-permute-start(bf16[2,64,512]{2,1,0:T(8,128)(2,1)S(1)} %get-tuple-element.33), channel_id=1, source_target_pairs={{0,12},{1,13},{2,14},{3,15},{4,8},{5,9},{6,10},{7,11},{8,4},{9,5},... | collective-permute-start | bytes 393224 | tf_op jit(solution)/shard_map/ppermute | solution.py:351
  8.9 17.4 %collective-permute-start.5 = (bf16[2,64,512]{2,1,0:T(8,128)(2,1)S(1)}, bf16[2,64,512]{2,1,0:T(8,128)(2,1)S(1)}, u32[]{:S(2)}, u32[]{:S(2)}) collective-permute-start(bf16[2,64,512]{2,1,0:T(8,128)(2,1)S(1)} %get-tuple-element.37), channel_id=1, source_target_pairs={{0,10},{1,11},{2,8},{3,9},{4,14},{5,15},{6,12},{7,13},{8,2},{9,3},... | collective-permute-start | bytes 393224 | tf_op jit(solution)/shard_map/ppermute | solution.py:351
  9.7 27.5 %collective-permute-start.2 = (bf16[4,64,512]{2,1,0:T(8,128)(2,1)S(1)}, bf16[4,64,512]{2,1,0:T(8,128)(2,1)S(1)}, u32[]{:S(2)}, u32[]{:S(2)}) collective-permute-start(bf16[4,64,512]{2,1,0:T(8,128)(2,1)S(1)} %get-tuple-element.34), channel_id=1, source_target_pairs={{0,6},{1,7},{2,4},{3,5},{4,2},{5,3},{6,0},{7,1},{8,14},{9,15},{10,... | collective-permute-start | bytes 786440 | tf_op jit(solution)/shard_map/ppermute | solution.py:351
  14.0 23.2 %collective-permute-start.3 = (bf16[4,64,512]{2,1,0:T(8,128)(2,1)S(1)}, bf16[4,64,512]{2,1,0:T(8,128)(2,1)S(1)}, u32[]{:S(2)}, u32[]{:S(2)}) collective-permute-start(bf16[4,64,512]{2,1,0:T(8,128)(2,1)S(1)} %get-tuple-element.35), channel_id=1, source_target_pairs={{0,4},{1,5},{2,6},{3,7},{4,0},{5,1},{6,2},{7,3},{8,12},{9,13},{10,... | collective-permute-start | bytes 786440 | tf_op jit(solution)/shard_map/ppermute | solution.py:351
  14.0 23.2 %collective-permute-start.4 = (bf16[4,64,512]{2,1,0:T(8,128)(2,1)S(1)}, bf16[4,64,512]{2,1,0:T(8,128)(2,1)S(1)}, u32[]{:S(2)}, u32[]{:S(2)}) collective-permute-start(bf16[4,64,512]{2,1,0:T(8,128)(2,1)S(1)} %get-tuple-element.36), channel_id=1, source_target_pairs={{0,2},{1,3},{2,0},{3,1},{4,6},{5,7},{6,4},{7,5},{8,10},{9,11},{10,... | collective-permute-start | bytes 786440 | tf_op jit(solution)/shard_map/ppermute | solution.py:351
  16.9 16.2 %collective-permute-start.6 = (bf16[2,64,512]{2,1,0:T(8,128)(2,1)S(1)}, bf16[2,64,512]{2,1,0:T(8,128)(2,1)S(1)}, u32[]{:S(2)}, u32[]{:S(2)}) collective-permute-start(bf16[2,64,512]{2,1,0:T(8,128)(2,1)S(1)} %get-tuple-element.38), channel_id=1, source_target_pairs={{0,8},{1,9},{2,10},{3,11},{4,12},{5,13},{6,14},{7,15},{8,0},{9,1},... | collective-permute-start | bytes 393224 | tf_op jit(solution)/shard_map/ppermute | solution.py:351
  26.4 10.8 %collective-permute-start.7 = (bf16[2,64,512]{2,1,0:T(8,128)(2,1)S(1)}, bf16[2,64,512]{2,1,0:T(8,128)(2,1)S(1)}, u32[]{:S(2)}, u32[]{:S(2)}) collective-permute-start(bf16[2,64,512]{2,1,0:T(8,128)(2,1)S(1)} %get-tuple-element.39), channel_id=1, source_target_pairs={{0,14},{1,15},{2,12},{3,13},{4,10},{5,11},{6,8},{7,9},{8,6},{9,7},... | collective-permute-start | bytes 393224 | tf_op jit(solution)/shard_map/ppermute | solution.py:351
  39.6 3.5 %collective-permute-start.8 = (bf16[12,2,64,512]{3,2,1,0:T(8,128)(2,1)S(1)}, bf16[12,2,64,512]{3,2,1,0:T(8,128)(2,1)S(1)}, u32[]{:S(2)}, u32[]{:S(2)}) collective-permute-start(bf16[12,2,64,512]{3,2,1,0:T(8,128)(2,1)S(1)} %join.2.refs_0_.refs_2_), channel_id=1, source_target_pairs={{0,1},{1,0},{2,3},{3,2},{4,5},{5,4},{6,7},{7,6},{8,9},{9,8},{10,11... | collective-permute-start | bytes 4718600 | tf_op jit(solution)/shard_map/ppermute | solution.py:351
  41.8 33.7 %copy-start.1 = (bf16[2,4,64,2048]{3,2,1,0:T(8,128)(2,1)S(1)}, bf16[2,4,64,2048]{3,2,1,0:T(8,128)(2,1)}, u32[]{:S(2)}) copy-start(bf16[2,4,64,2048]{3,2,1,0:T(8,128)(2,1)} %x_ref.5) | copy-start | bytes 6291460
  54.9 22.1 %copy-start.14 = (bf16[2,128,512]{2,1,0:T(8,128)(2,1)}, bf16[2,128,512]{2,1,0:T(8,128)(2,1)S(1)}, u32[]{:S(2)}) copy-start(bf16[2,128,512]{2,1,0:T(8,128)(2,1)S(1)} %get-tuple-element.48.refs_0_) | copy-start | bytes 786436
  54.9 22.1 %copy-start.16 = (bf16[2,128,512]{2,1,0:T(8,128)(2,1)}, bf16[2,128,512]{2,1,0:T(8,128)(2,1)S(1)}, u32[]{:S(2)}) copy-start(bf16[2,128,512]{2,1,0:T(8,128)(2,1)S(1)} %get-tuple-element.50) | copy-start | bytes 786436
  54.9 22.2 %copy-start.29 = (f32[2,3]{1,0:T(2,128)S(1)}, f32[2,3]{1,0:T(2,128)}, u32[]{:S(2)}) copy-start(f32[2,3]{1,0:T(2,128)} %param.12) | copy-start | bytes 76
  54.9 27.8 %copy-start.28 = (f32[1,3]{1,0:T(1,128)S(1)}, f32[1,3]{1,0:T(1,128)}, u32[]{:S(2)}) copy-start(f32[1,3]{1,0:T(1,128)} %constant.98) | copy-start | bytes 40
  54.9 20.6 %collective-permute-start.12 = (bf16[2,128,512]{2,1,0:T(8,128)(2,1)S(1)}, bf16[2,128,512]{2,1,0:T(8,128)(2,1)S(1)}, u32[]{:S(2)}, u32[]{:S(2)}) collective-permute-start(bf16[2,128,512]{2,1,0:T(8,128)(2,1)S(1)} %get-tuple-element.43), channel_id=1, source_target_pairs={{0,2},{1,3},{2,0},{3,1},{4,6},{5,7},{6,4},{7,5},{8,10},{9,11},{10,... | collective-permute-start | bytes 786440 | tf_op jit(solution)/shard_map/ppermute | solution.py:351
  56.4 8.2 %collective-permute-start.9 = (bf16[2,64,512]{2,1,0:T(8,128)(2,1)S(1)}, bf16[2,64,512]{2,1,0:T(8,128)(2,1)S(1)}, u32[]{:S(2)}, u32[]{:S(2)}) collective-permute-start(bf16[2,64,512]{2,1,0:T(8,128)(2,1)S(1)} %copy-done.23), channel_id=1, source_target_pairs={{0,12},{1,13},{2,14},{3,15},{4,8},{5,9},{6,10},{7,11},{8,4},{9,5},... | collective-permute-start | bytes 393224 | tf_op jit(solution)/shard_map/ppermute | solution.py:351
  58.4 15.7 %collective-permute-start.10 = (bf16[2,64,512]{2,1,0:T(8,128)(2,1)S(1)}, bf16[2,64,512]{2,1,0:T(8,128)(2,1)S(1)}, u32[]{:S(2)}, u32[]{:S(2)}) collective-permute-start(bf16[2,64,512]{2,1,0:T(8,128)(2,1)S(1)} %copy-done.21), channel_id=1, source_target_pairs={{0,10},{1,11},{2,8},{3,9},{4,14},{5,15},{6,12},{7,13},{8,2},{9,3},... | collective-permute-start | bytes 393224 | tf_op jit(solution)/shard_map/ppermute | solution.py:351
  58.6 16.9 %collective-permute-start.11 = (bf16[2,64,512]{2,1,0:T(8,128)(2,1)S(1)}, bf16[2,64,512]{2,1,0:T(8,128)(2,1)S(1)}, u32[]{:S(2)}, u32[]{:S(2)}) collective-permute-start(bf16[2,64,512]{2,1,0:T(8,128)(2,1)S(1)} %copy-done.19), channel_id=1, source_target_pairs={{0,8},{1,9},{2,10},{3,11},{4,12},{5,13},{6,14},{7,15},{8,0},{9,1},... | collective-permute-start | bytes 393224 | tf_op jit(solution)/shard_map/ppermute | solution.py:351
  77.0 5.7 %collective-permute-start.13 = (bf16[4,2,64,512]{3,2,1,0:T(8,128)(2,1)}, bf16[4,2,64,512]{3,2,1,0:T(8,128)(2,1)}, u32[]{:S(2)}, u32[]{:S(2)}) collective-permute-start(bf16[4,2,64,512]{3,2,1,0:T(8,128)(2,1)} %join.3.refs_2_), channel_id=1, source_target_pairs={{0,1},{1,0},{2,3},{3,2},{4,5},{5,4},{6,7},{7,6},{8,9},{9,8},{10,11... | collective-permute-start | bytes 1572872 | tf_op jit(solution)/shard_map/ppermute | solution.py:351
  80.3 18.5 %collective-permute-start.17 = (bf16[2,128,512]{2,1,0:T(8,128)(2,1)}, bf16[2,128,512]{2,1,0:T(8,128)(2,1)S(1)}, u32[]{:S(2)}, u32[]{:S(2)}) collective-permute-start(bf16[2,128,512]{2,1,0:T(8,128)(2,1)} %copy-done.17), channel_id=1, source_target_pairs={{0,4},{1,5},{2,6},{3,7},{4,0},{5,1},{6,2},{7,3},{8,12},{9,13},{10,... | collective-permute-start | bytes 786440 | tf_op jit(solution)/shard_map/ppermute | solution.py:351
  80.3 18.5 %collective-permute-start.18 = (bf16[2,128,512]{2,1,0:T(8,128)(2,1)}, bf16[2,128,512]{2,1,0:T(8,128)(2,1)S(1)}, u32[]{:S(2)}, u32[]{:S(2)}) collective-permute-start(bf16[2,128,512]{2,1,0:T(8,128)(2,1)} %copy-done.16), channel_id=1, source_target_pairs={{0,6},{1,7},{2,4},{3,5},{4,2},{5,3},{6,0},{7,1},{8,14},{9,15},{10,... | collective-permute-start | bytes 786440 | tf_op jit(solution)/shard_map/ppermute | solution.py:351
  95.2 9.4 %collective-permute-start.14 = (bf16[2,128,512]{2,1,0:T(8,128)(2,1)S(1)}, bf16[2,128,512]{2,1,0:T(8,128)(2,1)S(1)}, u32[]{:S(2)}, u32[]{:S(2)}) collective-permute-start(bf16[2,128,512]{2,1,0:T(8,128)(2,1)S(1)} %get-tuple-element.45), channel_id=1, source_target_pairs={{0,2},{1,3},{2,0},{3,1},{4,6},{5,7},{6,4},{7,5},{8,10},{9,11},{10,... | collective-permute-start | bytes 786440 | tf_op jit(solution)/shard_map/ppermute | solution.py:351
  96.4 9.2 %collective-permute-start.15 = (bf16[2,128,512]{2,1,0:T(8,128)(2,1)S(1)}, bf16[2,128,512]{2,1,0:T(8,128)(2,1)S(1)}, u32[]{:S(2)}, u32[]{:S(2)}) collective-permute-start(bf16[2,128,512]{2,1,0:T(8,128)(2,1)S(1)} %get-tuple-element.46), channel_id=1, source_target_pairs={{0,4},{1,5},{2,6},{3,7},{4,0},{5,1},{6,2},{7,3},{8,12},{9,13},{10,... | collective-permute-start | bytes 786440 | tf_op jit(solution)/shard_map/ppermute | solution.py:351
  96.5 13.7 %collective-permute-start.16 = (bf16[2,128,512]{2,1,0:T(8,128)(2,1)S(1)}, bf16[2,128,512]{2,1,0:T(8,128)(2,1)S(1)}, u32[]{:S(2)}, u32[]{:S(2)}) collective-permute-start(bf16[2,128,512]{2,1,0:T(8,128)(2,1)S(1)} %get-tuple-element.47), channel_id=1, source_target_pairs={{0,6},{1,7},{2,4},{3,5},{4,2},{5,3},{6,0},{7,1},{8,14},{9,15},{10,... | collective-permute-start | bytes 786440 | tf_op jit(solution)/shard_map/ppermute | solution.py:351
  116.3 18.9 %collective-permute-start.19 = (bf16[64,2048]{1,0:T(8,128)(2,1)S(1)}, bf16[64,2048]{1,0:T(8,128)(2,1)S(1)}, u32[]{:S(2)}, u32[]{:S(2)}) collective-permute-start(bf16[64,2048]{1,0:T(8,128)(2,1)S(1)} %get-tuple-element.53), channel_id=1, source_target_pairs={{0,8},{1,9},{2,10},{3,11},{4,12},{5,13},{6,14},{7,15},{8,0},{9,1},... | collective-permute-start | bytes 786440 | tf_op jit(solution)/shard_map/ppermute | solution.py:386
  117.4 7.2 %collective-permute-start.20 = (f32[16,1024]{1,0:T(8,128)S(1)}, f32[16,1024]{1,0:T(8,128)S(1)}, u32[]{:S(2)}, u32[]{:S(2)}) collective-permute-start(f32[16,1024]{1,0:T(8,128)S(1)} %get-tuple-element.55), channel_id=1, source_target_pairs={{0,1},{1,2},{2,3},{3,4},{4,5},{5,6},{6,7},{7,0},{8,9},{9,10},{10,1... | collective-permute-start | bytes 196616 | tf_op jit(solution)/shard_map/ppermute | solution.py:386
  117.5 7.2 %collective-permute-start.21 = (f32[16,1024]{1,0:T(8,128)S(1)}, f32[16,1024]{1,0:T(8,128)S(1)}, u32[]{:S(2)}, u32[]{:S(2)}) collective-permute-start(f32[16,1024]{1,0:T(8,128)S(1)} %get-tuple-element.56), channel_id=1, source_target_pairs={{0,7},{1,0},{2,1},{3,2},{4,3},{5,4},{6,5},{7,6},{8,15},{9,8},{10,9... | collective-permute-start | bytes 196616 | tf_op jit(solution)/shard_map/ppermute | solution.py:386
  120.1 7.2 %collective-permute-start.22 = (f32[16,1024]{1,0:T(8,128)S(1)}, f32[16,1024]{1,0:T(8,128)S(1)}, u32[]{:S(2)}, u32[]{:S(2)}) collective-permute-start(f32[16,1024]{1,0:T(8,128)S(1)} %get-tuple-element.57), channel_id=1, source_target_pairs={{0,9},{1,10},{2,11},{3,12},{4,13},{5,14},{6,15},{7,8},{8,1},{9,2},... | collective-permute-start | bytes 196616 | tf_op jit(solution)/shard_map/ppermute | solution.py:386
  120.1 15.1 %collective-permute-start.23 = (f32[16,1024]{1,0:T(8,128)S(1)}, f32[16,1024]{1,0:T(8,128)S(1)}, u32[]{:S(2)}, u32[]{:S(2)}) collective-permute-start(f32[16,1024]{1,0:T(8,128)S(1)} %get-tuple-element.58), channel_id=1, source_target_pairs={{0,15},{1,8},{2,9},{3,10},{4,11},{5,12},{6,13},{7,14},{8,7},{9,0},... | collective-permute-start | bytes 196616 | tf_op jit(solution)/shard_map/ppermute | solution.py:386
  (22 other events, 110.0 us)
